TPU v7x, 128 devices: a whole 4x4x4 slice. The times are simulated.
128 devices in a mesh: blk: 32 (over x, y, z_lo), rep: 4 (over z_hi, core).
Axes of the slice: x: 4, y: 4, z: 4 (z_hi: 2, z_lo: 2; z = z_hi * 2 + z_lo), core: 2. Of those that a mesh axis runs over, the one named last changes fastest.
Arguments:
- tile_values: bfloat16 [32, 4, 32, 1, 256, 256], P('blk', 'rep'), may hold values from -0.1875 to 0.1875
- tile_rows: int32 [32, 4, 32, 1], P('blk', 'rep'), may hold values from 0 to 1, as said below
- tile_cols: int32 [32, 4, 32, 1], P('blk', 'rep'), may hold values from 0 to 1
- tile_counts: int32 [32, 4, 32], P('blk', 'rep'), may hold values from 0 to 1, as said below
- grad_out: bfloat16 [16384, 512], P('blk'), may hold values from -6 to 6
- features: bfloat16 [16384, 512], P(('blk', 'rep')), may hold values from -0.125 to 0.125
- weight: bfloat16 [512, 512], replicated, may hold values from -0.25 to 0.25
Outputs:
- grad_features: float32 [16384, 512], P(('blk', 'rep'))
- grad_weight: float32 [512, 512], replicated
Inputs may be any that keep to these rules, and one draw needn't show every extreme that they name: `tile_counts`: every device has some column block with all 1 slots used. `tile_rows`: for each row block and column block, the slots of all devices of that row block lie at distinct tile positions.
All inputs are finite; a program needn't handle non-finite values.
Results may differ from a plain program's by a relative error of at most 0.0029.
Values may be sent and summed in bfloat16 or wider, within the bound.
A program may use at most 128 MiB of HBM per device.

v0:
```python
import jax
import jax.numpy as jnp
from jax import lax
from jax.sharding import PartitionSpec as P


def block_terms(values_here, selected, col_idx, count_here, per_row):
    product = jnp.einsum(
        "jsab,jsaf->jsbf", values_here, selected, preferred_element_type=jnp.float32
    )
    slot_iota = jnp.arange(values_here.shape[1])[None, :]
    valid = (slot_iota < count_here[:, None]).astype(jnp.float32)
    place = (col_idx[..., None] == jnp.arange(per_row)[None, None, :]).astype(jnp.float32) * valid[
        ..., None
    ]
    return jnp.einsum("jsc,jsbf->jcbf", place, product, precision=lax.Precision.HIGHEST)


def body(tile_values, tile_rows, tile_cols, tile_counts, grad_out, features, weight):
    values_here = tile_values[0, 0]
    row_idx = tile_rows[0, 0]
    col_idx = tile_cols[0, 0]
    count_here = tile_counts[0, 0]
    tile_side = values_here.shape[-1]
    blk_rows = grad_out.shape[0]
    width = grad_out.shape[1]
    per_row = blk_rows // tile_side
    g_flat = grad_out.reshape(per_row, tile_side, width)
    selected = g_flat[row_idx]
    term = block_terms(values_here, selected, col_idx, count_here, per_row)
    own_block = lax.psum_scatter(
        term.reshape(blk_rows * lax.axis_size("blk"), width), "blk", scatter_dimension=0, tiled=True
    )
    shared = lax.psum_scatter(own_block, "rep", scatter_dimension=0, tiled=True)
    rounded = shared.astype(jnp.bfloat16)
    grad_features = lax.dot_general(
        rounded, weight, (((1,), (1,)), ((), ())), preferred_element_type=jnp.float32
    )
    partial_weight = lax.dot_general(
        features, rounded, (((0,), (0,)), ((), ())), preferred_element_type=jnp.float32
    )
    grad_weight = lax.psum(partial_weight, ("blk", "rep"))
    return (grad_features, grad_weight)


def solution(mesh):
    placed = (
        P("blk", "rep", None, None, None, None),
        P("blk", "rep", None, None),
        P("blk", "rep", None, None),
        P("blk", "rep", None),
        P("blk", None),
        P(("blk", "rep"), None),
        P(),
    )
    return jax.shard_map(
        body, mesh=mesh, in_specs=placed, out_specs=(P(("blk", "rep"), None), P()), check_vma=False
    )
```

profile of v0, /device:TPU:1, one launch (start us, length us, event | category | flops | bytes accessed | tf_op | source)
XLA Modules:
  0.0 972.0 jit_solution(8976167498495208583)
XLA Ops:
  7.2 0.0 copy-start
  7.2 0.0 reduce-scatter.3.cloned.1.call-start
  7.2 0.7 fusion.6
  7.9 0.7 fusion.5
  8.6 0.0 copy-done
  8.6 4.9 gather_fusion
  13.5 12.7 %convolution_bitcast_fusion = f32[32,256,512]{1,2,0:T(8,128)} fusion(bf16[32,256,512]{2,1,0:T(8,128)(2,1)} %gather_fusion, bf16[1,1,32,1,256,256]{5,4,3,2,1,0:T(8,128)(2,1)} %param.7), kind=kOutput, calls=%fused_computation.2 | convolution fusion | flops 2147483648 | bytes 29360128 | tf_op jit(solution)/shard_map/jsab,jsaf->jsbf/dot_general | solution.py:8
  26.2 0.0 copy-start.4
  26.2 17.5 %copy.12 = f32[32,256,512]{2,1,0:T(8,128)} copy(f32[32,256,512]{1,2,0:T(8,128)} %convolution_bitcast_fusion) | data formatting | bytes 33554432 | tf_op jit(solution)/shard_map/jsab,jsaf->jsbf/dot_general | solution.py:8
  43.7 0.0 copy-done.4
  43.7 0.1 fusion.4
  43.7 19.0 %broadcast_multiply_fusion = f32[32,2,256,512]{3,2,1,0:T(8,128)} fusion(f32[32,256,512]{2,1,0:T(8,128)} %copy.12, f32[32,2]{1,0:T(8,128)S(1)} %fusion.4), kind=kLoop, calls=%fused_computation.1 | loop fusion | flops 8388608 | bytes 50331904 | tf_op jit(solution)/shard_map/jsc,jsbf->jcbf/dot_general | solution.py:16
  62.8 0.0 copy-start.3
  62.8 0.0 copy-start.2
  62.8 0.0 reduce-scatter.3.cloned.1.call-update
  62.8 0.0 copy-start.1
  62.8 0.0 reduce-scatter.5.cloned.1.call-start
  62.8 711.9 %reduce-scatter.3.cloned.1.call-done = f32[512,512]{1,0:T(8,128)} async-done(((f32[16384,512]{1,0:T(8,128)}), f32[512,512]{1,0:T(8,128)}) %reduce-scatter.3.cloned.1.call-update) | async-done | bytes 1048592 | tf_op jit(solution)/shard_map/reduce_scatter | solution.py:31
  774.8 0.0 reduce-scatter.5.cloned.1.call-update
  774.8 0.0 all-reduce.2.cloned.1.call-start
  774.9 35.4 %reduce-scatter.5.cloned.1.call-done = f32[128,512]{1,0:T(8,128)} async-done(((f32[512,512]{1,0:T(8,128)}), f32[128,512]{1,0:T(8,128)}) %reduce-scatter.5.cloned.1.call-update) | async-done | bytes 262160 | tf_op jit(solution)/shard_map/reduce_scatter | solution.py:34
  810.3 0.0 copy-done.3
  810.3 2.2 convolution_bitcast_fusion.1
  812.5 0.0 all-reduce.2.cloned.1.call-update
  812.5 0.0 copy-done.2
  812.5 2.0 fusion.2
  814.5 148.5 %all-reduce.2.cloned.1.call-done = f32[512,512]{0,1:T(8,128)} async-done(((f32[512,512]{0,1:T(8,128)}), f32[512,512]{0,1:T(8,128)}) %all-reduce.2.cloned.1.call-update) | async-done | bytes 1048592 | tf_op jit(solution)/shard_map/psum | solution.py:42
  963.0 2.5 copy.13
  965.5 0.0 copy-done.1
  (1 shorter events, 0.0 us)
Async XLA Ops:
  7.2 1.4 copy-start
  7.2 767.6 %reduce-scatter.3.cloned.1.call-start = ((), (), s32[]{:S(2)}) async-start(), calls=%async_computation.2 | async-start | bytes 34603008 | tf_op jit(solution)/shard_map/reduce_scatter | solution.py:31
  26.2 17.5 %copy-start.4 = (s32[1,1,32,1]{2,3,1,0:T(1,128)S(1)}, s32[1,1,32,1]{2,3,1,0:T(1,128)}, u32[]{:S(2)}) copy-start(s32[1,1,32,1]{2,3,1,0:T(1,128)} %param.9) | copy-start | bytes 388
  62.8 747.5 %copy-start.3 = (bf16[128,512]{1,0:T(8,128)(2,1)S(1)}, bf16[128,512]{1,0:T(8,128)(2,1)}, u32[]{:S(2)}) copy-start(bf16[128,512]{1,0:T(8,128)(2,1)} %param.12) | copy-start | bytes 393220
  62.8 749.8 %copy-start.2 = (bf16[512,512]{1,0:T(8,128)(2,1)S(1)}, bf16[512,512]{1,0:T(8,128)(2,1)}, u32[]{:S(2)}) copy-start(bf16[512,512]{1,0:T(8,128)(2,1)} %param.13) | copy-start | bytes 1572868
  62.8 902.7 %copy-start.1 = (bf16[512,512]{1,0:T(8,128)(2,1)S(1)}, bf16[512,512]{1,0:T(8,128)(2,1)}, u32[]{:S(2)}) copy-start(bf16[512,512]{1,0:T(8,128)(2,1)} %param.11) | copy-start | bytes 1572868
  62.8 747.5 %reduce-scatter.5.cloned.1.call-start = ((), (), s32[]{:S(2)}) async-start(), calls=%async_computation.3 | async-start | bytes 1310720 | tf_op jit(solution)/shard_map/reduce_scatter | solution.py:34
  774.8 188.2 %all-reduce.2.cloned.1.call-start = ((), (), s32[]{:S(2)}) async-start(), calls=%async_computation.4 | async-start | bytes 2097152 | tf_op jit(solution)/shard_map/psum | solution.py:42
Sparse Core Ops, SparseCore 0:
  62.9 711.8 reduce-scatter.2
  777.4 32.8 reduce-scatter.4
  816.4 146.5 all-reduce.1
where the time goes:
time: 973 us; the launch traced here: 972 us
  waiting for transfers between devices  896 us (92%)
  local copies, waits for them, and re-layouts  24.9 us (3%)
  other arithmetic  20.4 us (2%)
  matrix products  16.9 us (2%)
  between operations  13.8 us (1%)
    reduce_scatter x1, waiting for transfers between devices, body(): lax.psum_scatter(term.reshape(blk_rows * lax.axis_size('blk'), width), 'b...  712 us
    psum x1, waiting for transfers between devices, body(): grad_weight = lax.psum(partial_weight, ('blk', 'rep'))  148 us
    reduce_scatter x1, waiting for transfers between devices, body(): shared = lax.psum_scatter(own_block, 'rep', scatter_dimension=0, tiled=True)  35.4 us
  transfers between devices with their start and end apart: 3, of which 3 were waited for; matrix products, arithmetic and copies ran while one was open for 0% of the time, Pallas kernels for 0%

commit v1 on v0

v1 whole, which is shorter than its diff:
```python
import functools

import jax
import jax.numpy as jnp
from jax import lax
from jax.experimental import pallas as pl
from jax.experimental.pallas import tpu as pltpu
from jax.sharding import PartitionSpec as P

MESH = pl.DeviceIdType.MESH
F32 = jnp.float32
BF16 = jnp.bfloat16

ROWS = (176, 176, 160)
FIRST = (0, 176, 352)
X, Y, Z = 0, 1, 2
ORDERS = ((X, Z, Y), (Y, X, Z), (Z, Y, X))
QUARTER = (24, 24, 16)
QFIRST = (0, 96, 192)
GROUPS = ((0, 8), (8, 6), (14, 9), (23, 9))


def place(group, i):
    if group == 0:
        return 2, i // 2, i % 2
    if group == 1:
        return (i // 2 + 3) % 4, 2, i % 2
    return (i // 3 + 3) % 4, (i % 3 + 3) % 4, group - 2


def kernel(code_ref, tiles_ref, g_ref, x_ref, w_ref, gf_ref, gw_ref, *scratch):
    (t0, t1, code1, gt, xt, *rest) = scratch
    send = rest[0:3]
    full = rest[3:6]
    ra_m, ra_p, rb_m, rb_p = rest[6:9], rest[9:12], rest[12:15], rest[15:18]
    r2am, r2ap, r2bm, r2bp, r2fm, r2fp = (rest[18 + 3 * n : 21 + 3 * n] for n in range(6))
    r3am, r3ap, r3bm, r3bp, r3fm, r3fp = (rest[36 + 3 * n : 39 + 3 * n] for n in range(6))
    tot, gw, gwr, half, halfr = rest[54:59]
    x1, x2, x3 = rest[59:62], rest[62:65], rest[65:68]
    (tl, ts, tr, cs, cr, s1, ra, rb, s2, r2, s3, r3, es, er, xs, xr) = rest[68:]

    blk = lax.axis_index("blk")
    rep = lax.axis_index("rep")
    core = rep % 2
    pos = (blk // 8, (blk // 2) % 4, (rep // 2) * 2 + blk % 2)

    def device(where, which):
        return (where[0] * 8 + where[1] * 2 + where[2] % 2, (where[2] // 2) * 2 + which)

    def beside(axis, step):
        where = list(pos)
        where[axis] = (pos[axis] + step) % 4
        return device(where, core)

    partner = device(pos, 1 - core)

    def remote(src, dst, ssem, rsem, to):
        pltpu.make_async_remote_copy(
            src_ref=src, dst_ref=dst, send_sem=ssem, recv_sem=rsem, device_id=to, device_id_type=MESH
        ).start()

    def wait(ref, sem):
        pltpu.make_async_copy(ref, ref, sem).wait()

    def column(group, i):
        dx, dy, dl = place(group, i)
        return ((pos[0] + dx) % 4) * 8 + ((pos[1] + dy) % 4) * 2 + (pos[2] + dl) % 2

    mine = pl.ds(pl.multiple_of(core * 128, 128), 128)
    other = pl.ds(pl.multiple_of((1 - core) * 128, 128), 128)

    for group, (first, count) in enumerate(GROUPS):

        def load(i, carry, group=group, first=first):
            c = column(group, i)
            pltpu.make_async_copy(tiles_ref.at[c, :, mine], t0.at[first + i], tl.at[group]).start()
            return carry

        lax.fori_loop(0, count, load, 0)

    barrier = pltpu.get_barrier_semaphore()
    pl.semaphore_signal(barrier, inc=1, device_id=partner, device_id_type=MESH)
    for axis in (X, Y, Z):
        for step in (1, 2, 3):
            pl.semaphore_signal(barrier, inc=1, device_id=beside(axis, step), device_id_type=MESH)
    pl.semaphore_wait(barrier, 10)

    remote(code_ref, code1, cs, cr, partner)
    for group, (first, count) in enumerate(GROUPS):

        def swap(i, carry, group=group, first=first):
            c = column(group, i)
            remote(tiles_ref.at[c, :, other], t1.at[first + i], ts.at[group], tr.at[group], partner)
            return carry

        lax.fori_loop(0, count, swap, 0)

    gt[...] = g_ref[...].T
    xt[...] = x_ref[...].T
    wait(code1, cr)

    def products(group):
        first, count = GROUPS[group]
        wait(t0.at[first : first + count], tl.at[group])
        wait(t1.at[first : first + count], tr.at[group])

        def one(i, carry):
            dx, dy, dl = place(group, i)
            c = column(group, i)
            near = ((pos[2] + dl) % 4) // 2
            own, theirs = t0[first + i], t1[first + i]
            code_own = code_ref[pl.ds(c, 1), :]
            code_theirs = code1[pl.ds(c, 1), :]
            lines = []
            for row in range(2):
                line = []
                for col in (near, 1 - near):
                    key = (row * 2 + col).astype(F32)
                    keep_own = jnp.where(code_own == key, 1.0, 0.0).astype(BF16)
                    keep_theirs = jnp.where(code_theirs == key, 1.0, 0.0).astype(BF16)
                    line.append(own * keep_own + theirs * keep_theirs)
                lines.append(jnp.concatenate(line, axis=1))
            dense = jnp.concatenate(lines, axis=0)
            made = jnp.dot(gt[...], dense, preferred_element_type=F32)
            for part in range(3):
                rows = slice(FIRST[part], FIRST[part] + ROWS[part])
                for side in range(2):
                    block = made[rows, side * 128 : (side + 1) * 128]
                    rel = (dx, dy, dl + 2 * side)
                    at = tuple(rel[axis] for axis in ORDERS[part])
                    full[part][at] = block
                    send[part][at] = block.astype(BF16)
            return carry

        lax.fori_loop(0, count, one, 0)

    CHUNKS = (2, 1, 3, 0)

    def opposite1(part):
        axis = ORDERS[part][0]
        for t in CHUNKS:
            remote(send[part].at[2, t, 0:2], ra_m[part].at[t], s1.at[part, 0], ra.at[part, 0, t], beside(axis, 1))
            remote(send[part].at[2, t, 2:4], ra_p[part].at[t], s1.at[part, 0], ra.at[part, 1, t], beside(axis, 3))

    def plain1(part, t):
        axis = ORDERS[part][0]
        remote(send[part].at[1, t, 2:4], rb_m[part].at[t, 2:4], s1.at[part, 1], rb.at[part, 0, t], beside(axis, 1))
        remote(send[part].at[3, t, 0:2], rb_p[part].at[t, 0:2], s1.at[part, 2], rb.at[part, 1, t], beside(axis, 3))

    def merge1(part, t):
        axis = ORDERS[part][0]
        wait(ra_m[part].at[t], ra.at[part, 0, t])
        for b in range(2):
            send[part][1, t, b] = (full[part][1, t, b] + ra_m[part][t, b].astype(F32)).astype(BF16)
        remote(send[part].at[1, t, 0:2], rb_m[part].at[t, 0:2], s1.at[part, 1], rb.at[part, 0, t], beside(axis, 1))
        wait(ra_p[part].at[t], ra.at[part, 1, t])
        for b in range(2):
            send[part][3, t, 2 + b] = (full[part][3, t, 2 + b] + ra_p[part][t, b].astype(F32)).astype(BF16)
        remote(send[part].at[3, t, 2:4], rb_p[part].at[t, 2:4], s1.at[part, 2], rb.at[part, 1, t], beside(axis, 3))

    def sum1(part, t):
        wait(rb_m[part].at[t], rb.at[part, 0, t])
        wait(rb_p[part].at[t], rb.at[part, 1, t])

        def add(b, carry):
            total = full[part][0, t, b] + rb_m[part][t, b].astype(F32) + rb_p[part][t, b].astype(F32)
            full[part][0, t, b] = total
            send[part][0, t, b] = total.astype(BF16)
            return carry

        lax.fori_loop(0, 4, add, 0)

    products(0)
    opposite1(0)
    products(1)
    opposite1(1)
    products(2)
    opposite1(2)
    products(3)
    for t in CHUNKS:
        for part in range(3):
            plain1(part, t)
    for t in CHUNKS:
        for part in range(3):
            merge1(part, t)

    def merge2(part):
        axis = ORDERS[part][1]
        wait(r2am[part], r2.at[part, 0])
        for b in range(2):
            full[part][0, 1, b] = full[part][0, 1, b] + r2am[part][b].astype(F32)
        remote(full[part].at[0, 1, 0:2], r2fm[part], s2.at[part, 3], r2.at[part, 4], beside(axis, 1))
        wait(r2ap[part], r2.at[part, 1])
        for b in range(2):
            full[part][0, 3, 2 + b] = full[part][0, 3, 2 + b] + r2ap[part][b].astype(F32)
        remote(full[part].at[0, 3, 2:4], r2fp[part], s2.at[part, 4], r2.at[part, 5], beside(axis, 3))

    for t in CHUNKS:
        for part in range(3):
            axis = ORDERS[part][1]
            sum1(part, t)
            if t == 2:
                remote(send[part].at[0, 2, 0:2], r2am[part], s2.at[part, 0], r2.at[part, 0], beside(axis, 1))
                remote(send[part].at[0, 2, 2:4], r2ap[part], s2.at[part, 0], r2.at[part, 1], beside(axis, 3))
            if t == 1:
                remote(send[part].at[0, 1, 2:4], r2bm[part], s2.at[part, 1], r2.at[part, 2], beside(axis, 1))
            if t == 3:
                remote(send[part].at[0, 3, 0:2], r2bp[part], s2.at[part, 2], r2.at[part, 3], beside(axis, 3))
                merge2(part)

    for part in range(3):
        axis = ORDERS[part][2]
        mid, end = ROWS[part] // 2, ROWS[part]
        wait(r2fm[part], r2.at[part, 4])
        wait(r2bp[part], r2.at[part, 3])
        wait(r2bm[part], r2.at[part, 2])
        wait(r2fp[part], r2.at[part, 5])
        for b in (2, 1, 3, 0):
            if b < 2:
                arrived = r2fm[part][b] + r2bp[part][b].astype(F32)
            else:
                arrived = r2bm[part][b - 2].astype(F32) + r2fp[part][b - 2]
            full[part][0, 0, b] = full[part][0, 0, b] + arrived
            if b == 2:
                remote(full[part].at[0, 0, 2, 0:mid], r3am[part], s3.at[part, 0], r3.at[part, 0], beside(axis, 1))
                remote(full[part].at[0, 0, 2, mid:end], r3ap[part], s3.at[part, 1], r3.at[part, 1], beside(axis, 3))
            if b == 1:
                remote(full[part].at[0, 0, 1, mid:end], r3bm[part], s3.at[part, 2], r3.at[part, 2], beside(axis, 1))
            if b == 3:
                remote(full[part].at[0, 0, 3, 0:mid], r3bp[part], s3.at[part, 3], r3.at[part, 3], beside(axis, 3))
    for part in range(3):
        axis = ORDERS[part][2]
        mid, end = ROWS[part] // 2, ROWS[part]
        wait(r3am[part], r3.at[part, 0])
        full[part][0, 0, 1, 0:mid] = full[part][0, 0, 1, 0:mid] + r3am[part][...]
        remote(full[part].at[0, 0, 1, 0:mid], r3fm[part], s3.at[part, 4], r3.at[part, 4], beside(axis, 1))
        wait(r3ap[part], r3.at[part, 1])
        full[part][0, 0, 3, mid:end] = full[part][0, 0, 3, mid:end] + r3ap[part][...]
        remote(full[part].at[0, 0, 3, mid:end], r3fp[part], s3.at[part, 5], r3.at[part, 5], beside(axis, 3))
    for part in range(3):
        mid, end = ROWS[part] // 2, ROWS[part]
        at = FIRST[part]
        wait(r3bp[part], r3.at[part, 3])
        wait(r3fm[part], r3.at[part, 4])
        tot[at : at + mid] = full[part][0, 0, 0, 0:mid] + r3fm[part][...] + r3bp[part][...]
        wait(r3bm[part], r3.at[part, 2])
        wait(r3fp[part], r3.at[part, 5])
        tot[at + mid : at + end] = full[part][0, 0, 0, mid:end] + r3bm[part][...] + r3fp[part][...]

    total = tot[...].T
    high = total.astype(BF16)
    low = (total - high.astype(F32)).astype(BF16)

    gw[...] = jnp.dot(xt[...], high, preferred_element_type=F32) + jnp.dot(xt[...], low, preferred_element_type=F32)
    kept = pl.ds(pl.multiple_of(core * 256, 256), 256)
    given = pl.ds(pl.multiple_of((1 - core) * 256, 256), 256)
    remote(gw.at[given], gwr, es.at[0], er.at[0], partner)
    last = (((1,), (1,)), ((), ()))
    gf_ref[...] = lax.dot_general(high, w_ref[...], last, preferred_element_type=F32) + lax.dot_general(
        low, w_ref[...], last, preferred_element_type=F32
    )
    wait(gwr, er.at[0])
    half[...] = gw[kept, :] + gwr[...]

    for part in range(3):
        axis, size = ORDERS[part][0], QUARTER[part]
        for step in (2, 1, 3):
            quarter = pl.ds(pl.multiple_of(QFIRST[part] + ((pos[axis] + step) % 4) * size, 8), size)
            remote(half.at[quarter], x1[part].at[pos[axis]], xs.at[0, part], xr.at[0, part], beside(axis, step))
        x1[part][pos[axis]] = half[pl.ds(pl.multiple_of(QFIRST[part] + pos[axis] * size, 8), size), :]
    for stage, (took, gave) in enumerate(((x1, x2), (x2, x3))):
        for part in range(3):
            axis = ORDERS[part][stage + 1]
            wait(took[part].at[0:3], xr.at[stage, part])
            gave[part][pos[axis]] = (took[part][0] + took[part][1]) + (took[part][2] + took[part][3])
            for step in (2, 1, 3):
                here = gave[part].at[pos[axis]]
                remote(here, here, xs.at[stage + 1, part], xr.at[stage + 1, part], beside(axis, step))
    for part in range(3):
        axis, size = ORDERS[part][0], QUARTER[part]
        wait(x3[part].at[0:3], xr.at[2, part])
        wait(x1[part].at[0:3], xs.at[0, part])
        gwr[pl.ds(pl.multiple_of(QFIRST[part] + pos[axis] * size, 8), size), :] = (x3[part][0] + x3[part][1]) + (
            x3[part][2] + x3[part][3]
        )
        quarter = gwr.at[pl.ds(pl.multiple_of(QFIRST[part] + pos[axis] * size, 8), size)]
        for step in (2, 1, 3):
            remote(quarter, quarter, xs.at[3, part], xr.at[3, part], beside(axis, step))
    wait(gw.at[given], es.at[0])
    for part in range(3):
        size = QUARTER[part]
        wait(gwr.at[QFIRST[part] : QFIRST[part] + 3 * size], xr.at[3, part])
        rows = slice(QFIRST[part], QFIRST[part] + 4 * size)
        remote(gwr.at[rows], halfr.at[rows], es.at[1 + part], er.at[1 + part], partner)
    gw_ref[kept, :] = gwr[...]
    for part in range(3):
        size = QUARTER[part]
        rows = slice(QFIRST[part], QFIRST[part] + 4 * size)
        wait(halfr.at[rows], er.at[1 + part])
    gw_ref[given, :] = halfr[...]

    wait(code_ref, cs)
    for group, (first, count) in enumerate(GROUPS):
        wait(t1.at[first : first + count], ts.at[group])
    for part in range(3):
        mid, end = ROWS[part] // 2, ROWS[part]
        for n, region in enumerate((2, 1, 3)):
            wait(send[part].at[region], s1.at[part, n])
        wait(send[part].at[0, 2], s2.at[part, 0])
        wait(send[part].at[0, 1, 2:4], s2.at[part, 1])
        wait(send[part].at[0, 3, 0:2], s2.at[part, 2])
        wait(full[part].at[0, 1, 0:2], s2.at[part, 3])
        wait(full[part].at[0, 3, 2:4], s2.at[part, 4])
        for n in range(6):
            wait(r3am[part], s3.at[part, n])
        for stage in (1, 2):
            wait(x2[part].at[0:3], xs.at[stage, part])
        size = QUARTER[part]
        wait(gwr.at[QFIRST[part] : QFIRST[part] + 3 * size], xs.at[3, part])
        rows = slice(QFIRST[part], QFIRST[part] + 4 * size)
        wait(gwr.at[rows], es.at[1 + part])


def body(tile_values, tile_rows, tile_cols, tile_counts, grad_out, features, weight):
    tiles = tile_values[0, 0, :, 0]
    spot = tile_rows[0, 0, :, 0] * 2 + tile_cols[0, 0, :, 0]
    code = jnp.where(tile_counts[0, 0] > 0, spot, -1).astype(F32)
    code = jnp.broadcast_to(code[:, None], (32, 128))
    vmem = pl.BlockSpec(memory_space=pltpu.VMEM)

    def per_part(*shape, dtype, rows=ROWS, lanes=128):
        return [pltpu.VMEM((*shape, r, lanes), dtype) for r in rows]

    halves = tuple(r // 2 for r in ROWS)
    dma = pltpu.SemaphoreType.DMA
    scratch = [
        pltpu.VMEM((32, 256, 128), BF16),
        pltpu.VMEM((32, 256, 128), BF16),
        pltpu.VMEM((32, 128), F32),
        pltpu.VMEM((512, 512), BF16),
        pltpu.VMEM((512, 128), BF16),
        *per_part(4, 4, 4, dtype=BF16),
        *per_part(4, 4, 4, dtype=F32),
        *per_part(4, 2, dtype=BF16),
        *per_part(4, 2, dtype=BF16),
        *per_part(4, 4, dtype=BF16),
        *per_part(4, 4, dtype=BF16),
        *per_part(2, dtype=BF16),
        *per_part(2, dtype=BF16),
        *per_part(2, dtype=BF16),
        *per_part(2, dtype=BF16),
        *per_part(2, dtype=F32),
        *per_part(2, dtype=F32),
    ]
    for _ in range(6):
        scratch += per_part(dtype=F32, rows=halves)
    scratch += [
        pltpu.VMEM((512, 128), F32),
        pltpu.VMEM((512, 512), F32),
        pltpu.VMEM((256, 512), F32),
        pltpu.VMEM((256, 512), F32),
        pltpu.VMEM((256, 512), F32),
    ]
    for _ in range(3):
        scratch += per_part(4, dtype=F32, rows=QUARTER, lanes=512)
    scratch += [
        dma((4,)),
        dma((4,)),
        dma((4,)),
        dma,
        dma,
        dma((3, 3)),
        dma((3, 2, 4)),
        dma((3, 2, 4)),
        dma((3, 5)),
        dma((3, 6)),
        dma((3, 6)),
        dma((3, 6)),
        dma((4,)),
        dma((4,)),
        dma((4, 3)),
        dma((4, 3)),
    ]
    return pl.pallas_call(
        kernel,
        out_shape=(jax.ShapeDtypeStruct((128, 512), F32), jax.ShapeDtypeStruct((512, 512), F32)),
        in_specs=[vmem, pl.BlockSpec(memory_space=pl.ANY), vmem, vmem, vmem],
        out_specs=(vmem, vmem),
        scratch_shapes=scratch,
        compiler_params=pltpu.CompilerParams(
            collective_id=0, has_side_effects=True, vmem_limit_bytes=56 * 1024 * 1024
        ),
    )(code, tiles, grad_out, features, weight)


def solution(mesh):
    placed = (
        P("blk", "rep", None, None, None, None),
        P("blk", "rep", None, None),
        P("blk", "rep", None, None),
        P("blk", "rep", None),
        P("blk", None),
        P(("blk", "rep"), None),
        P(),
    )
    return jax.shard_map(
        body, mesh=mesh, in_specs=placed, out_specs=(P(("blk", "rep"), None), P()), check_vma=False
    )
```

time: 973 us -> 91 us (0.09)
  waiting for transfers between devices: 896 us -> 0 us
  Pallas kernels: 0 us -> 84.9 us
  local copies, waits for them, and re-layouts: 24.9 us -> 4.61 us
  other arithmetic: 20.4 us -> 0.69 us
  matrix products: 16.9 us -> 0 us
  between operations: 13.8 us -> 0.64 us
    reduce_scatter x2 -> x0, waiting for transfers between devices: 747 us -> none  [the longest x1 712 us: body(): lax.psum_scatter(term.reshape(blk_rows * lax.axis_size('blk'), width), 'b...]
    psum x1 -> x0, waiting for transfers between devices: 148 us -> none  [body(): grad_weight = lax.psum(partial_weight, ('blk', 'rep'))]
    pallas_call x0 -> x1, Pallas kernels: none -> 84.9 us  [body(): pl.pallas_call(kernel, out_shape=(jax.ShapeDtypeStruct((128, 512), F32),...]
    dot_general x1 -> x0, other arithmetic: 19 us -> none  [block_terms(): jnp.einsum('jsc,jsbf->jcbf', place, product, precision=lax.Precision.HIGH...]
    dot_general x1 -> x0, local copies, waits for them, and re-layouts: 17.5 us -> none  [block_terms(): jnp.einsum('jsab,jsaf->jsbf', values_here, selected, preferred_element_ty...]
    dot_general x3 -> x0, matrix products: 16.9 us -> none  [the longest x1 12.7 us: block_terms(): jnp.einsum('jsab,jsaf->jsbf', values_here, selected, preferred_element_ty...]
  transfers between devices with their start and end apart: 3 -> 0, of which waited for: 3 -> 0; matrix products, arithmetic and copies ran while one was open for 0% -> 0% of each run, Pallas kernels for 0% -> 0%
where the time goes in v1:
time: 91 us; the launch traced here: 90.8 us
  Pallas kernels  84.9 us (93%)
  local copies, waits for them, and re-layouts  4.61 us (5%)
    pallas_call x1, Pallas kernels, body(): pl.pallas_call(kernel, out_shape=(jax.ShapeDtypeStruct((128, 512), F32),...  84.9 us
    unnamed x2, local copies, waits for them, and re-layouts  3.93 us

profile of v1, /device:TPU:1, one launch (start us, length us, event | category | flops | bytes accessed | tf_op | source)
XLA Modules:
  0.0 90.8 jit_solution(17446538201704260919)
XLA Ops:
  0.6 0.7 fusion
  1.3 0.7 broadcast_in_dim.11.code_ref
  2.0 84.9 %shard_map.86 = (f32[128,512]{1,0:T(8,128)}, f32[512,512]{1,0:T(8,128)}) custom-call(f32[32,128]{1,0:T(8,128)} %broadcast_in_dim.11.code_ref, bf16[32,256,256]{2,1,0:T(8,128)(2,1)} %bitcast.7, bf16[512,512]{1,0:T(8,128)(2,1)} %g_ref.1, bf16[128,512]{1,0:T(8,128)(2,1)} %x_ref.1, bf16[512,512]{1,0:T(8,128)(2,1)} %w_ref.1), custom_call_target="tpu_custom_call" | custom-call | tf_op jit(solution)/shard_map/pallas_call | solution.py:384
  86.9 1.7 %copy.11 = f32[128,512]{1,0:T(8,128)} copy(f32[128,512]{1,0:T(8,128)} %get-tuple-element.4) | data formatting | bytes 524288
  88.6 2.3 %copy.12 = f32[512,512]{1,0:T(8,128)} copy(f32[512,512]{1,0:T(8,128)} %get-tuple-element.5) | data formatting | bytes 2097152

commit v2 on v1

v2 whole, which is shorter than its diff:
```python
import functools

import jax
import jax.numpy as jnp
from jax import lax
from jax.experimental import pallas as pl
from jax.experimental.pallas import tpu as pltpu
from jax.sharding import PartitionSpec as P

MESH = pl.DeviceIdType.MESH
F32 = jnp.float32
BF16 = jnp.bfloat16

ROWS = (176, 176, 160)
FIRST = (0, 176, 352)
X, Y, Z = 0, 1, 2
ORDERS = ((X, Z, Y), (Y, X, Z), (Z, Y, X))
QUARTER = (24, 24, 16)
QFIRST = (0, 96, 192)
GROUPS = ((0, 8), (8, 6), (14, 9), (23, 9))


def place(group, i):
    if group == 0:
        return 2, (i // 2 + 2) % 4, i % 2
    if group == 1:
        return (i // 2 + 3) % 4, 2, i % 2
    return (i // 3 + 3) % 4, (i % 3 + 3) % 4, group - 2


def kernel(rows_ref, cols_ref, counts_ref, tiles_ref, g_any, x_any, w_any, gf_any, gw_any, *scratch):
    (t0, t1, code0, code1, g_ref, x_ref, w_ref, gf, gt, xt, *rest) = scratch
    send = rest[0:3]
    full = rest[3:6]
    ra, rb = rest[6:9], rest[9:12]
    r2am, r2ap, r2bm, r2bp, r2fm, r2fp = (rest[12 + 3 * n : 15 + 3 * n] for n in range(6))
    r3am, r3ap, r3bm, r3bp, r3fm, r3fp = (rest[30 + 3 * n : 33 + 3 * n] for n in range(6))
    tot, gw, gwr, half, halfr, halfp = rest[48:54]
    x1, x2, x3 = rest[54:57], rest[57:60], rest[60:63]
    (ins, outs, tl, ts, tr, cs, cr, s1, ras, rbs, s2, r2, s3, r3, es, er, xs, xr, fs, fr) = rest[63:]

    blk = lax.axis_index("blk")
    rep = lax.axis_index("rep")
    core = rep % 2
    pos = (blk // 8, (blk // 2) % 4, (rep // 2) * 2 + blk % 2)

    def device(where, which):
        return (where[0] * 8 + where[1] * 2 + where[2] % 2, (where[2] // 2) * 2 + which)

    def beside(axis, step):
        where = list(pos)
        where[axis] = (pos[axis] + step) % 4
        return device(where, core)

    partner = device(pos, 1 - core)

    def remote(src, dst, ssem, rsem, to):
        pltpu.make_async_remote_copy(
            src_ref=src, dst_ref=dst, send_sem=ssem, recv_sem=rsem, device_id=to, device_id_type=MESH
        ).start()

    def wait(ref, sem):
        pltpu.make_async_copy(ref, ref, sem).wait()

    def column(group, i):
        dx, dy, dl = place(group, i)
        return ((pos[0] + dx) % 4) * 8 + ((pos[1] + dy) % 4) * 2 + (pos[2] + dl) % 2

    mine = pl.ds(pl.multiple_of(core * 128, 128), 128)
    other = pl.ds(pl.multiple_of((1 - core) * 128, 128), 128)

    for group, (first, count) in enumerate(GROUPS):

        def load(i, carry, group=group, first=first):
            c = column(group, i)
            pltpu.make_async_copy(tiles_ref.at[c, :, mine], t0.at[first + i], tl.at[group]).start()
            return carry

        lax.fori_loop(0, count, load, 0)

    def fetch(src, dst, sem):
        copy = pltpu.make_async_copy(src, dst, sem)
        copy.start()
        return copy

    get_g = fetch(g_any, g_ref, ins.at[0])
    get_x = fetch(x_any, x_ref, ins.at[1])
    get_w = fetch(w_any, w_ref, ins.at[2])

    sent = []

    def finish():
        for region, sem in sent:
            wait(region, sem)

    barrier = pltpu.get_barrier_semaphore()
    pl.semaphore_signal(barrier, inc=1, device_id=partner, device_id_type=MESH)
    for axis in (X, Y, Z):
        for step in (1, 2, 3):
            pl.semaphore_signal(barrier, inc=1, device_id=beside(axis, step), device_id_type=MESH)
    for c in range(32):
        spot = rows_ref[0, 0, c] * 2 + cols_ref[0, 0, c]
        used = jnp.where(counts_ref[0, 0, c] > 0, spot, -1)
        code0[c : c + 1, :] = jnp.full((1, 128), used, jnp.int32).astype(F32)
    get_g.wait()
    gt[...] = g_ref[...].T
    pl.semaphore_wait(barrier, 10)

    remote(code0, code1, cs, cr, partner)
    sent.append((code0, cs))
    for group, (first, count) in enumerate(GROUPS):

        def swap(i, carry, group=group, first=first):
            c = column(group, i)
            remote(tiles_ref.at[c, :, other], t1.at[first + i], ts.at[group], tr.at[group], partner)
            return carry

        lax.fori_loop(0, count, swap, 0)
        sent.append((t1.at[first : first + count], ts.at[group]))

    get_x.wait()
    xt[...] = x_ref[...].T
    wait(code1, cr)

    def send1(part, at1, at2, at3):
        axis = ORDERS[part][0]
        opposite = (at1 // 2) * (1 - at1 % 2)
        way = opposite * (at3 // 2) + (1 - opposite) * (at1 // 2)
        plain = (at1 % 2) * ((at1 // 2 + at3 // 2) % 2)
        block = send[part].at[at1, at2, at3]
        to = beside(axis, 1 + 2 * way)

        @pl.when(opposite == 1)
        def _():
            remote(block, ra[part].at[way, at2, at3 % 2], s1.at[part, at1], ras.at[part, way, at2], to)

        @pl.when(plain == 1)
        def _():
            remote(block, rb[part].at[way, at2, at3], s1.at[part, at1], rbs.at[part, way, at2], to)

    def products(group):
        first, count = GROUPS[group]
        wait(t0.at[first : first + count], tl.at[group])
        wait(t1.at[first : first + count], tr.at[group])

        def one(i, carry):
            dx, dy, dl = place(group, i)
            c = column(group, i)
            near = ((pos[2] + dl) % 4) // 2
            own, theirs = t0[first + i], t1[first + i]
            code_own = code0[pl.ds(c, 1), :]
            code_theirs = code1[pl.ds(c, 1), :]
            lines = []
            for row in range(2):
                line = []
                for col in (near, 1 - near):
                    key = (row * 2 + col).astype(F32)
                    keep_own = jnp.where(code_own == key, 1.0, 0.0).astype(BF16)
                    keep_theirs = jnp.where(code_theirs == key, 1.0, 0.0).astype(BF16)
                    line.append(own * keep_own + theirs * keep_theirs)
                lines.append(jnp.concatenate(line, axis=1))
            dense = jnp.concatenate(lines, axis=0)
            made = jnp.dot(gt[...], dense, preferred_element_type=F32)
            for part in range(3):
                rows = slice(FIRST[part], FIRST[part] + ROWS[part])
                for side in range(2):
                    block = made[rows, side * 128 : (side + 1) * 128]
                    rel = (dx, dy, dl + 2 * side)
                    at = tuple(rel[axis] for axis in ORDERS[part])
                    full[part][at] = block
                    send[part][at] = block.astype(BF16)
            for part in range(3):
                for side in range(2):
                    rel = (dx, dy, dl + 2 * side)
                    send1(part, *(rel[axis] for axis in ORDERS[part]))
            return carry

        lax.fori_loop(0, count, one, 0)

    def merge1(part, t):
        axis = ORDERS[part][0]
        for way, at1, low in ((0, 1, 0), (1, 3, 2)):
            wait(ra[part].at[way, t], ras.at[part, way, t])
            for b in range(2):
                send[part][at1, t, low + b] = (full[part][at1, t, low + b] + ra[part][way, t, b].astype(F32)).astype(BF16)
            pair = slice(low, low + 2)
            remote(
                send[part].at[at1, t, pair],
                rb[part].at[way, t, pair],
                s1.at[part, at1],
                rbs.at[part, way, t],
                beside(axis, 1 + 2 * way),
            )

    def sum1(part, t):
        wait(rb[part].at[0, t], rbs.at[part, 0, t])
        wait(rb[part].at[1, t], rbs.at[part, 1, t])

        def add(b, carry):
            total = full[part][0, t, b] + rb[part][0, t, b].astype(F32) + rb[part][1, t, b].astype(F32)
            full[part][0, t, b] = total
            send[part][0, t, b] = total.astype(BF16)
            return carry

        lax.fori_loop(0, 4, add, 0)

    def merge2(part):
        axis = ORDERS[part][1]
        wait(r2am[part], r2.at[part, 0])
        for b in range(2):
            full[part][0, 1, b] = full[part][0, 1, b] + r2am[part][b].astype(F32)
        remote(full[part].at[0, 1, 0:2], r2fm[part], s2.at[part, 3], r2.at[part, 4], beside(axis, 1))
        wait(r2ap[part], r2.at[part, 1])
        for b in range(2):
            full[part][0, 3, 2 + b] = full[part][0, 3, 2 + b] + r2ap[part][b].astype(F32)
        remote(full[part].at[0, 3, 2:4], r2fp[part], s2.at[part, 4], r2.at[part, 5], beside(axis, 3))

    def step2(part, t):
        axis = ORDERS[part][1]
        sum1(part, t)
        if t == 2:
            remote(send[part].at[0, 2, 0:2], r2am[part], s2.at[part, 0], r2.at[part, 0], beside(axis, 1))
            remote(send[part].at[0, 2, 2:4], r2ap[part], s2.at[part, 0], r2.at[part, 1], beside(axis, 3))
        if t == 1:
            remote(send[part].at[0, 1, 2:4], r2bm[part], s2.at[part, 1], r2.at[part, 2], beside(axis, 1))
        if t == 3:
            remote(send[part].at[0, 3, 0:2], r2bp[part], s2.at[part, 2], r2.at[part, 3], beside(axis, 3))

    products(0)
    products(1)
    merge1(1, 2)
    products(2)
    merge1(2, 2)
    merge1(0, 2)
    products(3)
    for t in (1, 3):
        for part in (1, 2, 0):
            merge1(part, t)
    for part in (1, 2, 0):
        step2(part, 2)
        merge1(part, 0)
    for part in (1, 2, 0):
        step2(part, 1)
    for part in (1, 2, 0):
        step2(part, 3)
        merge2(part)
    for part in (1, 2, 0):
        step2(part, 0)
    for part in range(3):
        for at1 in (1, 2, 3):
            sent.append((send[part].at[at1], s1.at[part, at1]))
        sent.append((send[part].at[0, 2], s2.at[part, 0]))
        sent.append((send[part].at[0, 1, 2:4], s2.at[part, 1]))
        sent.append((send[part].at[0, 3, 0:2], s2.at[part, 2]))
        sent.append((full[part].at[0, 1, 0:2], s2.at[part, 3]))
        sent.append((full[part].at[0, 3, 2:4], s2.at[part, 4]))

    for part in range(3):
        axis = ORDERS[part][2]
        mid, end = ROWS[part] // 2, ROWS[part]
        wait(r2fm[part], r2.at[part, 4])
        wait(r2bp[part], r2.at[part, 3])
        wait(r2bm[part], r2.at[part, 2])
        wait(r2fp[part], r2.at[part, 5])
        for b in (2, 1, 3, 0):
            if b < 2:
                arrived = r2fm[part][b] + r2bp[part][b].astype(F32)
            else:
                arrived = r2bm[part][b - 2].astype(F32) + r2fp[part][b - 2]
            full[part][0, 0, b] = full[part][0, 0, b] + arrived
            if b == 2:
                remote(full[part].at[0, 0, 2, 0:mid], r3am[part], s3.at[part, 0], r3.at[part, 0], beside(axis, 1))
                remote(full[part].at[0, 0, 2, mid:end], r3ap[part], s3.at[part, 1], r3.at[part, 1], beside(axis, 3))
            if b == 1:
                remote(full[part].at[0, 0, 1, mid:end], r3bm[part], s3.at[part, 2], r3.at[part, 2], beside(axis, 1))
            if b == 3:
                remote(full[part].at[0, 0, 3, 0:mid], r3bp[part], s3.at[part, 3], r3.at[part, 3], beside(axis, 3))
    for part in range(3):
        axis = ORDERS[part][2]
        mid, end = ROWS[part] // 2, ROWS[part]
        wait(r3am[part], r3.at[part, 0])
        full[part][0, 0, 1, 0:mid] = full[part][0, 0, 1, 0:mid] + r3am[part][...]
        remote(full[part].at[0, 0, 1, 0:mid], r3fm[part], s3.at[part, 4], r3.at[part, 4], beside(axis, 1))
        wait(r3ap[part], r3.at[part, 1])
        full[part][0, 0, 3, mid:end] = full[part][0, 0, 3, mid:end] + r3ap[part][...]
        remote(full[part].at[0, 0, 3, mid:end], r3fp[part], s3.at[part, 5], r3.at[part, 5], beside(axis, 3))
    for part in range(3):
        mid, end = ROWS[part] // 2, ROWS[part]
        at = FIRST[part]
        wait(r3bp[part], r3.at[part, 3])
        wait(r3fm[part], r3.at[part, 4])
        tot[at : at + mid] = full[part][0, 0, 0, 0:mid] + r3fm[part][...] + r3bp[part][...]
        wait(r3bm[part], r3.at[part, 2])
        wait(r3fp[part], r3.at[part, 5])
        tot[at + mid : at + end] = full[part][0, 0, 0, mid:end] + r3bm[part][...] + r3fp[part][...]

    for part in range(3):
        for n in range(6):
            sent.append((r3am[part], s3.at[part, n]))

    total = tot[...].T
    high = total.astype(BF16)
    low = (total - high.astype(F32)).astype(BF16)

    kept = pl.ds(pl.multiple_of(core * 256, 256), 256)
    given = pl.ds(pl.multiple_of((1 - core) * 256, 256), 256)
    for rows in (given, kept):
        left = xt[rows, :]
        gw[rows, :] = jnp.dot(left, high, preferred_element_type=F32) + jnp.dot(left, low, preferred_element_type=F32)
        if rows is given:
            remote(gw.at[given], gwr, es, er, partner)
    sent.append((gwr, es))
    wait(gwr, er)
    half[...] = gw[kept, :] + gwr[...]

    for part in range(3):
        axis, size = ORDERS[part][0], QUARTER[part]
        for step in (2, 1, 3):
            quarter = pl.ds(pl.multiple_of(QFIRST[part] + ((pos[axis] + step) % 4) * size, 8), size)
            remote(half.at[quarter], x1[part].at[pos[axis]], xs.at[0, part], xr.at[0, part], beside(axis, step))
        x1[part][pos[axis]] = half[pl.ds(pl.multiple_of(QFIRST[part] + pos[axis] * size, 8), size), :]
        sent.append((x1[part].at[0:3], xs.at[0, part]))
    get_w.wait()
    last = (((1,), (1,)), ((), ()))
    gf[...] = lax.dot_general(high, w_ref[...], last, preferred_element_type=F32) + lax.dot_general(
        low, w_ref[...], last, preferred_element_type=F32
    )
    out_f = fetch(gf, gf_any, outs.at[0])
    for part in range(3):
        axis = ORDERS[part][1]
        wait(x1[part].at[0:3], xr.at[0, part])
        x1[part][0] = (x1[part][0] + x1[part][1]) + (x1[part][2] + x1[part][3])
        for step in (2, 1, 3):
            lanes = pl.ds(pl.multiple_of(((pos[axis] + step) % 4) * 128, 128), 128)
            remote(x1[part].at[0, :, lanes], x2[part].at[pos[axis]], xs.at[1, part], xr.at[1, part], beside(axis, step))
        x2[part][pos[axis]] = x1[part][0, :, pl.ds(pl.multiple_of(pos[axis] * 128, 128), 128)]
        sent.append((x2[part].at[0:3], xs.at[1, part]))
    for part in range(3):
        axis = ORDERS[part][2]
        wait(x2[part].at[0:3], xr.at[1, part])
        x3[part][pos[axis]] = (x2[part][0] + x2[part][1]) + (x2[part][2] + x2[part][3])
        for step in (2, 1, 3):
            here = x3[part].at[pos[axis]]
            remote(here, here, xs.at[2, part], xr.at[2, part], beside(axis, step))
        sent.append((x3[part].at[0:3], xs.at[2, part]))
    for part in range(3):
        axis, size = ORDERS[part][1], QUARTER[part]
        wait(x3[part].at[0:3], xr.at[2, part])
        lanes = pl.ds(pl.multiple_of(pos[axis] * 128, 128), 128)
        rows = pl.ds(pl.multiple_of(QFIRST[part] + pos[ORDERS[part][0]] * size, 8), size)
        halfr[rows, lanes] = (x3[part][0] + x3[part][1]) + (x3[part][2] + x3[part][3])
        here = halfr.at[rows, lanes]
        for step in (2, 1, 3):
            remote(here, here, xs.at[3, part], xr.at[3, part], beside(axis, step))
        sent.append((x3[part].at[0:3], xs.at[3, part]))

    puts = []
    for part in range(3):
        axis, size = ORDERS[part][0], QUARTER[part]
        wait(x3[part].at[0:3], xr.at[3, part])
        rows = pl.ds(pl.multiple_of(QFIRST[part] + pos[axis] * size, 8), size)
        here = halfr.at[rows]
        for step in (2, 1, 3):
            remote(here, here, xs.at[4, part], xr.at[4, part], beside(axis, step))
        remote(here, halfp.at[rows], fs.at[0, part], fr.at[0, part], partner)
        sent.append((halfr.at[0 : 3 * size], xs.at[4, part]))
        sent.append((halfr.at[0:size], fs.at[0, part]))
    for part in range(3):
        axis, size = ORDERS[part][0], QUARTER[part]
        wait(halfr.at[0 : 3 * size], xr.at[4, part])
        for step in (1, 2, 3):
            rows = pl.ds(pl.multiple_of(QFIRST[part] + ((pos[axis] + step) % 4) * size, 8), size)
            remote(halfr.at[rows], halfp.at[rows], fs.at[1, part], fr.at[1, part], partner)
        sent.append((halfr.at[0 : 3 * size], fs.at[1, part]))
    puts.append(fetch(halfr, gw_any.at[kept], outs.at[1]))
    for part in range(3):
        size = QUARTER[part]
        wait(halfr.at[0:size], fr.at[0, part])
        wait(halfr.at[0 : 3 * size], fr.at[1, part])
    puts.append(fetch(halfp, gw_any.at[given], outs.at[2]))
    for put in puts:
        put.wait()
    out_f.wait()
    finish()


def deliver(gf_from, gw_from, gf_to, gw_to, gf, gw, ins, outs):
    pieces = [(gf_from, gf, gf_to)]
    for n in range(4):
        rows = pl.ds(128 * n, 128)
        pieces.append((gw_from.at[rows], gw.at[rows], gw_to.at[rows]))
    gets = [pltpu.make_async_copy(src, mid, ins.at[n]) for n, (src, mid, _) in enumerate(pieces)]
    puts = [pltpu.make_async_copy(mid, dst, outs.at[n]) for n, (_, mid, dst) in enumerate(pieces)]
    for get in gets:
        get.start()
    for get, put in zip(gets, puts):
        get.wait()
        put.start()
    for put in puts:
        put.wait()


def body(tile_values, tile_rows, tile_cols, tile_counts, grad_out, features, weight):
    tiles = tile_values[0, 0, :, 0]
    anywhere = pl.BlockSpec(memory_space=pl.ANY)
    smem = pl.BlockSpec(memory_space=pltpu.SMEM)

    def per_part(*shape, dtype, rows=ROWS, lanes=128):
        return [pltpu.VMEM((*shape, r, lanes), dtype) for r in rows]

    halves = tuple(r // 2 for r in ROWS)
    dma = pltpu.SemaphoreType.DMA
    scratch = [
        pltpu.VMEM((32, 256, 128), BF16),
        pltpu.VMEM((32, 256, 128), BF16),
        pltpu.VMEM((32, 128), F32),
        pltpu.VMEM((32, 128), F32),
        pltpu.VMEM((512, 512), BF16),
        pltpu.VMEM((128, 512), BF16),
        pltpu.VMEM((512, 512), BF16),
        pltpu.VMEM((128, 512), F32),
        pltpu.VMEM((512, 512), BF16),
        pltpu.VMEM((512, 128), BF16),
        *per_part(4, 4, 4, dtype=BF16),
        *per_part(4, 4, 4, dtype=F32),
        *per_part(2, 4, 2, dtype=BF16),
        *per_part(2, 4, 4, dtype=BF16),
        *per_part(2, dtype=BF16),
        *per_part(2, dtype=BF16),
        *per_part(2, dtype=BF16),
        *per_part(2, dtype=BF16),
        *per_part(2, dtype=F32),
        *per_part(2, dtype=F32),
    ]
    for _ in range(6):
        scratch += per_part(dtype=F32, rows=halves)
    scratch += [
        pltpu.VMEM((512, 128), F32),
        pltpu.VMEM((512, 512), F32),
        pltpu.VMEM((256, 512), F32),
        pltpu.VMEM((256, 512), F32),
        pltpu.VMEM((256, 512), F32),
        pltpu.VMEM((256, 512), F32),
    ]
    for lanes in (512, 128, 128):
        scratch += per_part(4, dtype=F32, rows=QUARTER, lanes=lanes)
    scratch += [
        dma((3,)),
        dma((3,)),
        dma((4,)),
        dma((4,)),
        dma((4,)),
        dma,
        dma,
        dma((3, 4)),
        dma((3, 2, 4)),
        dma((3, 2, 4)),
        dma((3, 5)),
        dma((3, 6)),
        dma((3, 6)),
        dma((3, 6)),
        dma,
        dma,
        dma((5, 3)),
        dma((5, 3)),
        dma((2, 3)),
        dma((2, 3)),
    ]
    outputs = (jax.ShapeDtypeStruct((128, 512), F32), jax.ShapeDtypeStruct((512, 512), F32))
    made = pl.pallas_call(
        kernel,
        out_shape=outputs,
        in_specs=[smem, smem, smem, anywhere, anywhere, anywhere, anywhere],
        out_specs=(anywhere, anywhere),
        scratch_shapes=scratch,
        compiler_params=pltpu.CompilerParams(
            collective_id=0, has_side_effects=True, vmem_limit_bytes=56 * 1024 * 1024
        ),
    )(tile_rows[..., 0], tile_cols[..., 0], tile_counts, tiles, grad_out, features, weight)
    return pl.pallas_call(
        deliver,
        out_shape=outputs,
        in_specs=[anywhere, anywhere],
        out_specs=(anywhere, anywhere),
        scratch_shapes=[pltpu.VMEM((128, 512), F32), pltpu.VMEM((512, 512), F32), dma((5,)), dma((5,))],
    )(*made)


def solution(mesh):
    placed = (
        P("blk", "rep", None, None, None, None),
        P("blk", "rep", None, None),
        P("blk", "rep", None, None),
        P("blk", "rep", None),
        P("blk", None),
        P(("blk", "rep"), None),
        P(),
    )
    return jax.shard_map(
        body, mesh=mesh, in_specs=placed, out_specs=(P(("blk", "rep"), None), P()), check_vma=False
    )
```

time: 91 us -> 82.8 us (0.910)
  local copies, waits for them, and re-layouts: 4.61 us -> 0 us
  Pallas kernels: 84.9 us -> 82 us
    unnamed x2 -> x0, local copies, waits for them, and re-layouts: 3.93 us -> none
    pallas_call x1 -> x2, Pallas kernels: 84.9 us -> 82 us  [the longest x1 79.9 us: body(): pl.pallas_call(kernel, out_shape=outputs, in_specs=[smem, smem, smem, any...]
where the time goes in v2:
time: 82.8 us; the launch traced here: 82.6 us
  Pallas kernels  82 us (99%)
    pallas_call x1, Pallas kernels, body(): pl.pallas_call(kernel, out_shape=outputs, in_specs=[smem, smem, smem, any...  79.9 us
    pallas_call x1, Pallas kernels, body(): pl.pallas_call(deliver, out_shape=outputs, in_specs=[anywhere, anywhere],...  2.08 us

profile of v2, /device:TPU:1, one launch (start us, length us, event | category | flops | bytes accessed | tf_op | source)
XLA Modules:
  0.0 82.6 jit_solution(7497081296794649517)
XLA Ops:
  0.6 79.9 %shard_map.86 = (f32[128,512]{1,0:T(8,128)}, f32[512,512]{1,0:T(8,128)}) custom-call(s32[1,1,32]{2,1,0:T(1,128)} %bitcast.4, s32[1,1,32]{2,1,0:T(1,128)} %bitcast.5, s32[1,1,32]{2,1,0:T(1,128)} %counts_ref.1, bf16[32,256,256]{2,1,0:T(8,128)(2,1)} %bitcast.3, bf16[512,512]{1,0:T(8,128)(2,1)} %g_any.1, bf16[128,512]{1,0:T(8,128)(2,1)} %x_any.1, ...), custom_call_target="tpu_custom_call" | custom-call | tf_op jit(solution)/shard_map/pallas_call | solution.py:470
  80.5 2.1 %shard_map.87 = (f32[128,512]{1,0:T(8,128)}, f32[512,512]{1,0:T(8,128)}) custom-call(f32[128,512]{1,0:T(8,128)} %get-tuple-element.4.gf_from, f32[512,512]{1,0:T(8,128)} %get-tuple-element.5.gw_from), custom_call_target="tpu_custom_call" | custom-call | tf_op jit(solution)/shard_map/pallas_call | solution.py:480

commit v3 on v2

v3 whole, which is shorter than its diff:
```python
import functools

import jax
import jax.numpy as jnp
from jax import lax
from jax.experimental import pallas as pl
from jax.experimental.pallas import tpu as pltpu
from jax.sharding import PartitionSpec as P

MESH = pl.DeviceIdType.MESH
F32 = jnp.float32
BF16 = jnp.bfloat16

ROWS = (176, 176, 160)
FIRST = (0, 176, 352)
X, Y, Z = 0, 1, 2
ORDERS = ((X, Z, Y), (Y, X, Z), (Z, Y, X))
QUARTER = (24, 24, 16)
QFIRST = (0, 96, 192)
GROUPS = ((0, 2), (2, 6), (8, 6), (14, 9), (23, 9))


def place(group, i):
    if group == 0:
        return 2, 2 + 0 * i, i
    if group == 1:
        return 2, (i // 2 + 3) % 4, i % 2
    if group == 2:
        return (i // 2 + 3) % 4, 2, i % 2
    return (i // 3 + 3) % 4, (i % 3 + 3) % 4, group - 3


def kernel(rows_ref, cols_ref, counts_ref, tiles_ref, g_any, x_any, w_any, gf, gw_out, *scratch):
    (t0, t1, code0, code1, g_ref, w_ref, gt, xg, *rest) = scratch
    send = rest[0:3]
    full = rest[3:6]
    ra, rb, rc, rd = rest[6:9], rest[9:12], rest[12:15], rest[15:18]
    tot, gw, gwr, half = rest[18:22]
    x1, x2, x3 = rest[22:25], rest[25:28], rest[28:31]
    (ins, gs, gr, tl, ts, tr, cs, cr, s1, ras, rbs, s2, r2, s3, r3, es, er, xs, xr, fs, fr) = rest[31:]

    blk = lax.axis_index("blk")
    rep = lax.axis_index("rep")
    core = rep % 2
    pos = (blk // 8, (blk // 2) % 4, (rep // 2) * 2 + blk % 2)

    def device(where, which):
        return (where[0] * 8 + where[1] * 2 + where[2] % 2, (where[2] // 2) * 2 + which)

    def beside(axis, step):
        where = list(pos)
        where[axis] = (pos[axis] + step) % 4
        return device(where, core)

    partner = device(pos, 1 - core)

    def remote(src, dst, ssem, rsem, to):
        pltpu.make_async_remote_copy(
            src_ref=src, dst_ref=dst, send_sem=ssem, recv_sem=rsem, device_id=to, device_id_type=MESH
        ).start()

    def wait(ref, sem):
        pltpu.make_async_copy(ref, ref, sem).wait()

    def column(group, i):
        dx, dy, dl = place(group, i)
        return ((pos[0] + dx) % 4) * 8 + ((pos[1] + dy) % 4) * 2 + (pos[2] + dl) % 2

    mine = pl.ds(pl.multiple_of(core * 128, 128), 128)
    other = pl.ds(pl.multiple_of((1 - core) * 128, 128), 128)

    for group, (first, count) in enumerate(GROUPS):

        def load(i, carry, group=group, first=first):
            c = column(group, i)
            pltpu.make_async_copy(tiles_ref.at[c, :, mine], t0.at[first + i], tl.at[group]).start()
            return carry

        lax.fori_loop(0, count, load, 0)

    def fetch(src, dst, sem):
        copy = pltpu.make_async_copy(src, dst, sem)
        copy.start()
        return copy

    get_g = fetch(g_any, g_ref, ins.at[0])
    get_x = [fetch(x_any, xg.at[axis, 3], ins.at[1 + axis]) for axis in (X, Y, Z)]
    get_w = fetch(w_any, w_ref, ins.at[4])

    sent = []

    def finish():
        for region, sem in sent:
            wait(region, sem)

    barrier = pltpu.get_barrier_semaphore()
    pl.semaphore_signal(barrier, inc=1, device_id=partner, device_id_type=MESH)
    for axis in (X, Y, Z):
        for step in (1, 2, 3):
            pl.semaphore_signal(barrier, inc=1, device_id=beside(axis, step), device_id_type=MESH)
    for c in range(32):
        spot = rows_ref[0, 0, c] * 2 + cols_ref[0, 0, c]
        used = jnp.where(counts_ref[0, 0, c] > 0, spot, -1)
        code0[c : c + 1, :] = jnp.full((1, 128), used, jnp.int32).astype(F32)
    get_g.wait()
    gt[...] = g_ref[...].T
    for get in get_x:
        get.wait()
    pl.semaphore_wait(barrier, 10)

    remote(code0, code1, cs, cr, partner)
    sent.append((code0, cs))
    for group, (first, count) in enumerate(GROUPS):

        def swap(i, carry, group=group, first=first):
            c = column(group, i)
            remote(tiles_ref.at[c, :, other], t1.at[first + i], ts.at[group], tr.at[group], partner)
            return carry

        lax.fori_loop(0, count, swap, 0)
        sent.append((t1.at[first : first + count], ts.at[group]))
        if group == 0:
            for axis in (X, Y, Z):
                for step in (2, 1, 3):
                    remote(xg.at[axis, 3], xg.at[axis, step - 1], gs.at[axis], gr.at[axis], beside(axis, step))
                sent.append((xg.at[axis, 0:3], gs.at[axis]))

    wait(code1, cr)

    def send1(part, at1, at2, at3):
        axis = ORDERS[part][0]
        opposite = (at1 // 2) * (1 - at1 % 2)
        way = opposite * (at3 // 2) + (1 - opposite) * (at1 // 2)
        plain = (at1 % 2) * ((at1 // 2 + at3 // 2) % 2)
        block = send[part].at[at1, at2, at3]
        to = beside(axis, 1 + 2 * way)

        @pl.when(opposite == 1)
        def _():
            remote(block, ra[part].at[way, at2, at3 % 2], s1.at[part, at1], ras.at[part, way, at2], to)

        @pl.when(plain == 1)
        def _():
            remote(block, rb[part].at[way, at2, at3], s1.at[part, at1], rbs.at[part, way, at2], to)

    def products(group):
        first, count = GROUPS[group]
        wait(t0.at[first : first + count], tl.at[group])
        wait(t1.at[first : first + count], tr.at[group])

        def one(i, carry):
            dx, dy, dl = place(group, i)
            c = column(group, i)
            near = ((pos[2] + dl) % 4) // 2
            own, theirs = t0[first + i], t1[first + i]
            code_own = code0[pl.ds(c, 1), :]
            code_theirs = code1[pl.ds(c, 1), :]
            lines = []
            for row in range(2):
                line = []
                for col in (near, 1 - near):
                    key = (row * 2 + col).astype(F32)
                    keep_own = jnp.where(code_own == key, 1.0, 0.0).astype(BF16)
                    keep_theirs = jnp.where(code_theirs == key, 1.0, 0.0).astype(BF16)
                    line.append(own * keep_own + theirs * keep_theirs)
                lines.append(jnp.concatenate(line, axis=1))
            dense = jnp.concatenate(lines, axis=0)
            made = jnp.dot(gt[...], dense, preferred_element_type=F32)
            for part in range(3):
                rows = slice(FIRST[part], FIRST[part] + ROWS[part])
                for side in range(2):
                    block = made[rows, side * 128 : (side + 1) * 128]
                    rel = (dx, dy, dl + 2 * side)
                    at = tuple(rel[axis] for axis in ORDERS[part])
                    full[part][at] = block
                    send[part][at] = block.astype(BF16)
            for part in range(3):
                for side in range(2):
                    rel = (dx, dy, dl + 2 * side)
                    send1(part, *(rel[axis] for axis in ORDERS[part]))
            return carry

        lax.fori_loop(0, count, one, 0)

    def merge1(part, t):
        axis = ORDERS[part][0]
        for way, at1, low in ((0, 1, 0), (1, 3, 2)):
            wait(ra[part].at[way, t], ras.at[part, way, t])
            for b in range(2):
                send[part][at1, t, low + b] = (full[part][at1, t, low + b] + ra[part][way, t, b].astype(F32)).astype(BF16)
            pair = slice(low, low + 2)
            remote(
                send[part].at[at1, t, pair],
                rb[part].at[way, t, pair],
                s1.at[part, at1],
                rbs.at[part, way, t],
                beside(axis, 1 + 2 * way),
            )

    def sum1(part, t):
        wait(rb[part].at[0, t], rbs.at[part, 0, t])
        wait(rb[part].at[1, t], rbs.at[part, 1, t])

        def add(b, carry):
            total = full[part][0, t, b] + rb[part][0, t, b].astype(F32) + rb[part][1, t, b].astype(F32)
            full[part][0, t, b] = total
            send[part][0, t, b] = total.astype(BF16)
            return carry

        lax.fori_loop(0, 4, add, 0)

    def step2(part, t):
        axis = ORDERS[part][1]
        sum1(part, t)
        if t > 0:
            remote(send[part].at[0, t], rc[part].at[t - 1], s2.at[part, t - 1], r2.at[part, t - 1], beside(axis, t))

    products(0)
    products(1)
    products(2)
    merge1(1, 2)
    products(3)
    merge1(2, 2)
    merge1(0, 2)
    products(4)
    for t in (1, 3):
        for part in (1, 2, 0):
            merge1(part, t)
    for part in (1, 2, 0):
        step2(part, 2)
        merge1(part, 0)
    for t in (1, 3, 0):
        for part in (1, 2, 0):
            step2(part, t)
    for part in range(3):
        for at1 in (1, 2, 3):
            sent.append((send[part].at[at1], s1.at[part, at1]))
        for t in (1, 2, 3):
            sent.append((send[part].at[0, t], s2.at[part, t - 1]))

    def split(value):
        high = value.astype(BF16)
        return high, (value - high.astype(F32)).astype(BF16)

    for part in (1, 2, 0):
        axis = ORDERS[part][2]
        for t in range(3):
            wait(rc[part].at[t], r2.at[part, t])
        for b in (2, 1, 3, 0):
            near, far, back = (rc[part][t, b].astype(F32) for t in range(3))
            full[part][0, 0, b] = (full[part][0, 0, b] + near) + (far + back)
            if b > 0:
                remote(full[part].at[0, 0, b], rd[part].at[b - 1], s3.at[part, b - 1], r3.at[part, b - 1], beside(axis, b))
        wait(xg.at[axis, 0:3], gr.at[axis])
        high, low = split(jnp.concatenate([full[part][0, 0, b] for b in (3, 2, 1, 0)], axis=1))
        owners = xg[axis].reshape(512, 512)
        gw[FIRST[part] : FIRST[part] + ROWS[part]] = jnp.dot(high, owners, preferred_element_type=F32) + jnp.dot(
            low, owners, preferred_element_type=F32
        )

    kept = pl.ds(pl.multiple_of(core * 256, 256), 256)
    given = pl.ds(pl.multiple_of((1 - core) * 256, 256), 256)
    remote(gw.at[given], gwr, es, er, partner)
    sent.append((gwr, es))
    wait(gwr, er)
    half[...] = gw[kept, :] + gwr[...]

    for part in range(3):
        axis, size = ORDERS[part][0], QUARTER[part]
        for step in (2, 1, 3):
            quarter = pl.ds(pl.multiple_of(QFIRST[part] + ((pos[axis] + step) % 4) * size, 8), size)
            remote(half.at[quarter], x1[part].at[pos[axis]], xs.at[0, part], xr.at[0, part], beside(axis, step))
        x1[part][pos[axis]] = half[pl.ds(pl.multiple_of(QFIRST[part] + pos[axis] * size, 8), size), :]
        sent.append((x1[part].at[0:3], xs.at[0, part]))
    for part in (1, 2, 0):
        for b in range(3):
            wait(rd[part].at[b], r3.at[part, b])
            sent.append((rd[part].at[b], s3.at[part, b]))
        rows = slice(FIRST[part], FIRST[part] + ROWS[part])
        tot[rows] = (full[part][0, 0, 0] + rd[part][0]) + (rd[part][1] + rd[part][2])
    high, low = split(tot[...].T)
    get_w.wait()
    last = (((1,), (1,)), ((), ()))
    gf[...] = lax.dot_general(high, w_ref[...], last, preferred_element_type=F32) + lax.dot_general(
        low, w_ref[...], last, preferred_element_type=F32
    )
    for part in range(3):
        axis = ORDERS[part][1]
        wait(x1[part].at[0:3], xr.at[0, part])
        x1[part][0] = (x1[part][0] + x1[part][1]) + (x1[part][2] + x1[part][3])
        for step in (2, 1, 3):
            lanes = pl.ds(pl.multiple_of(((pos[axis] + step) % 4) * 128, 128), 128)
            remote(x1[part].at[0, :, lanes], x2[part].at[pos[axis]], xs.at[1, part], xr.at[1, part], beside(axis, step))
        x2[part][pos[axis]] = x1[part][0, :, pl.ds(pl.multiple_of(pos[axis] * 128, 128), 128)]
        sent.append((x2[part].at[0:3], xs.at[1, part]))
    for part in range(3):
        axis = ORDERS[part][2]
        wait(x2[part].at[0:3], xr.at[1, part])
        x3[part][pos[axis]] = (x2[part][0] + x2[part][1]) + (x2[part][2] + x2[part][3])
        for step in (2, 1, 3):
            here = x3[part].at[pos[axis]]
            remote(here, here, xs.at[2, part], xr.at[2, part], beside(axis, step))
        sent.append((x3[part].at[0:3], xs.at[2, part]))
    for part in range(3):
        axis, size = ORDERS[part][1], QUARTER[part]
        wait(x3[part].at[0:3], xr.at[2, part])
        lanes = pl.ds(pl.multiple_of(pos[axis] * 128, 128), 128)
        rows = pl.ds(pl.multiple_of(core * 256 + QFIRST[part] + pos[ORDERS[part][0]] * size, 8), size)
        gw_out[rows, lanes] = (x3[part][0] + x3[part][1]) + (x3[part][2] + x3[part][3])
        here = gw_out.at[rows, lanes]
        for step in (2, 1, 3):
            remote(here, here, xs.at[3, part], xr.at[3, part], beside(axis, step))
        sent.append((x3[part].at[0:3], xs.at[3, part]))

    for part in range(3):
        axis, size = ORDERS[part][0], QUARTER[part]
        wait(x3[part].at[0:3], xr.at[3, part])
        rows = pl.ds(pl.multiple_of(core * 256 + QFIRST[part] + pos[axis] * size, 8), size)
        here = gw_out.at[rows]
        for step in (2, 1, 3):
            remote(here, here, xs.at[4, part], xr.at[4, part], beside(axis, step))
        remote(here, here, fs.at[0, part], fr.at[0, part], partner)
        sent.append((half.at[0 : 3 * size], xs.at[4, part]))
        sent.append((half.at[0:size], fs.at[0, part]))
    for part in range(3):
        axis, size = ORDERS[part][0], QUARTER[part]
        wait(half.at[0 : 3 * size], xr.at[4, part])
        for step in (1, 2, 3):
            first = core * 256 + QFIRST[part] + ((pos[axis] + step) % 4) * size
            here = gw_out.at[pl.ds(pl.multiple_of(first, 8), size)]
            remote(here, here, fs.at[1, part], fr.at[1, part], partner)
        sent.append((half.at[0 : 3 * size], fs.at[1, part]))
    for part in range(3):
        size = QUARTER[part]
        wait(half.at[0:size], fr.at[0, part])
        wait(half.at[0 : 3 * size], fr.at[1, part])
    finish()


def body(tile_values, tile_rows, tile_cols, tile_counts, grad_out, features, weight):
    tiles = tile_values[0, 0, :, 0]
    anywhere = pl.BlockSpec(memory_space=pl.ANY)
    smem = pl.BlockSpec(memory_space=pltpu.SMEM)

    def per_part(*shape, dtype, rows=ROWS, lanes=128):
        return [pltpu.VMEM((*shape, r, lanes), dtype) for r in rows]

    dma = pltpu.SemaphoreType.DMA
    scratch = [
        pltpu.VMEM((32, 256, 128), BF16),
        pltpu.VMEM((32, 256, 128), BF16),
        pltpu.VMEM((32, 128), F32),
        pltpu.VMEM((32, 128), F32),
        pltpu.VMEM((512, 512), BF16),
        pltpu.VMEM((512, 512), BF16),
        pltpu.VMEM((512, 512), BF16),
        pltpu.VMEM((3, 4, 128, 512), BF16),
        *per_part(4, 4, 4, dtype=BF16),
        *per_part(4, 4, 4, dtype=F32),
        *per_part(2, 4, 2, dtype=BF16),
        *per_part(2, 4, 4, dtype=BF16),
        *per_part(3, 4, dtype=BF16),
        *per_part(3, dtype=F32),
        pltpu.VMEM((512, 128), F32),
        pltpu.VMEM((512, 512), F32),
        pltpu.VMEM((256, 512), F32),
        pltpu.VMEM((256, 512), F32),
    ]
    for lanes in (512, 128, 128):
        scratch += per_part(4, dtype=F32, rows=QUARTER, lanes=lanes)
    scratch += [
        dma((5,)),
        dma((3,)),
        dma((3,)),
        dma((5,)),
        dma((5,)),
        dma((5,)),
        dma,
        dma,
        dma((3, 4)),
        dma((3, 2, 4)),
        dma((3, 2, 4)),
        dma((3, 3)),
        dma((3, 3)),
        dma((3, 3)),
        dma((3, 3)),
        dma,
        dma,
        dma((5, 3)),
        dma((5, 3)),
        dma((2, 3)),
        dma((2, 3)),
    ]
    vmem = pl.BlockSpec(memory_space=pltpu.VMEM)
    grad_features, turned = pl.pallas_call(
        kernel,
        out_shape=(pltpu.VMEM((128, 512), F32), pltpu.VMEM((512, 512), F32)),
        in_specs=[smem, smem, smem, anywhere, anywhere, anywhere, anywhere],
        out_specs=(vmem, vmem),
        scratch_shapes=scratch,
        compiler_params=pltpu.CompilerParams(
            collective_id=0, has_side_effects=True, vmem_limit_bytes=56 * 1024 * 1024
        ),
    )(tile_rows[..., 0], tile_cols[..., 0], tile_counts, tiles, grad_out, features, weight)
    return grad_features, turned.T


def solution(mesh):
    placed = (
        P("blk", "rep", None, None, None, None),
        P("blk", "rep", None, None),
        P("blk", "rep", None, None),
        P("blk", "rep", None),
        P("blk", None),
        P(("blk", "rep"), None),
        P(),
    )
    return jax.shard_map(
        body, mesh=mesh, in_specs=placed, out_specs=(P(("blk", "rep"), None), P()), check_vma=False
    )
```

time: 82.8 us -> 77.3 us (0.934)
  Pallas kernels: 82 us -> 74.5 us
  local copies, waits for them, and re-layouts: 0 us -> 2.01 us
    pallas_call x2 -> x1, Pallas kernels: 82 us -> 74.5 us  [body(): pl.pallas_call(kernel, out_shape=(pltpu.VMEM((128, 512), F32), pltpu.VMEM...]
    unnamed x0 -> x2, local copies, waits for them, and re-layouts: none -> 2.01 us
where the time goes in v3:
time: 77.3 us; the launch traced here: 77.2 us
  Pallas kernels  74.5 us (96%)
  local copies, waits for them, and re-layouts  2.01 us (3%)
    pallas_call x1, Pallas kernels, body(): pl.pallas_call(kernel, out_shape=(pltpu.VMEM((128, 512), F32), pltpu.VMEM...  74.5 us
    unnamed x2, local copies, waits for them, and re-layouts  2.01 us

profile of v3, /device:TPU:1, one launch (start us, length us, event | category | flops | bytes accessed | tf_op | source)
XLA Modules:
  0.0 77.2 jit_solution(15901317581450104938)
XLA Ops:
  0.6 74.5 %shard_map.86 = (f32[128,512]{1,0:T(8,128)S(1)}, f32[512,512]{1,0:T(8,128)S(1)}) custom-call(s32[1,1,32]{2,1,0:T(1,128)} %bitcast.6, s32[1,1,32]{2,1,0:T(1,128)} %bitcast.7, s32[1,1,32]{2,1,0:T(1,128)} %counts_ref.1, bf16[32,256,256]{2,1,0:T(8,128)(2,1)} %bitcast.5, bf16[512,512]{1,0:T(8,128)(2,1)} %g_any.1, bf16[128,512]{1,0:T(8,128)(2,1)} %x_any.1, ...), custom_call_target="tpu_custom_call" | custom-call | tf_op jit(solution)/shard_map/pallas_call | solution.py:395
  75.2 0.7 copy.11
  75.9 1.3 %copy.9 = f32[512,512]{1,0:T(8,128)} copy(f32[512,512]{0,1:T(8,128)S(1)} %bitcast.4) | data formatting | bytes 2097152

commit v4 on v3

v4 whole, which is shorter than its diff:
```python
import functools

import jax
import jax.numpy as jnp
from jax import lax
from jax.experimental import pallas as pl
from jax.experimental.pallas import tpu as pltpu
from jax.sharding import PartitionSpec as P

MESH = pl.DeviceIdType.MESH
F32 = jnp.float32
BF16 = jnp.bfloat16

ROWS = (176, 176, 160)
FIRST = (0, 176, 352)
X, Y, Z = 0, 1, 2
ORDERS = ((X, Z, Y), (Y, X, Z), (Z, Y, X))
QUARTER = (48, 48, 32)
QFIRST = (0, 192, 384)
PLACES = (2, 1, 3, 0)


def kernel(rows_ref, cols_ref, counts_ref, tiles_ref, g_any, x_any, w_any, gf, gw_out, *scratch):
    (t0, t1, code0, code1, g_ref, w_ref, gt, xg, *rest) = scratch
    send = rest[0:3]
    full = rest[3:6]
    ra, rb, rc, rd = rest[6:9], rest[9:12], rest[12:15], rest[15:18]
    tot, gw, gwr, half = rest[18:22]
    x1, x2, x3 = rest[22:25], rest[25:28], rest[28:31]
    (ins, gs, gr, tl, ts, tr, cs, cr, s1, ras, rbs, rps, s2, r2, s3, r3, es, er, xs, xr, fs, fr) = rest[31:]

    blk = lax.axis_index("blk")
    rep = lax.axis_index("rep")
    core = rep % 2
    pos = (blk // 8, (blk // 2) % 4, (rep // 2) * 2 + blk % 2)

    def device(where, which):
        return (where[0] * 8 + where[1] * 2 + where[2] % 2, (where[2] // 2) * 2 + which)

    def beside(axis, step):
        where = list(pos)
        where[axis] = (pos[axis] + step) % 4
        return device(where, core)

    partner = device(pos, 1 - core)

    def remote(src, dst, ssem, rsem, to):
        pltpu.make_async_remote_copy(
            src_ref=src, dst_ref=dst, send_sem=ssem, recv_sem=rsem, device_id=to, device_id_type=MESH
        ).start()

    def wait(ref, sem):
        pltpu.make_async_copy(ref, ref, sem).wait()

    mine = pl.ds(pl.multiple_of(core * 128, 128), 128)
    other = pl.ds(pl.multiple_of((1 - core) * 128, 128), 128)

    def columns(n):
        return pl.ds(((pos[0] + PLACES[n]) % 4) * 8, 8)

    for n in range(4):
        pltpu.make_async_copy(tiles_ref.at[columns(n), :, mine], t0.at[8 * n : 8 * n + 8], tl.at[n]).start()

    def fetch(src, dst, sem):
        copy = pltpu.make_async_copy(src, dst, sem)
        copy.start()
        return copy

    get_g = fetch(g_any, g_ref, ins.at[0])
    get_x = [fetch(x_any, xg.at[axis, 3], ins.at[1 + axis]) for axis in (X, Y, Z)]
    get_w = fetch(w_any, w_ref, ins.at[4])

    sent = []

    def finish():
        for region, sem in sent:
            wait(region, sem)

    barrier = pltpu.get_barrier_semaphore()
    pl.semaphore_signal(barrier, inc=1, device_id=partner, device_id_type=MESH)
    for axis in (X, Y, Z):
        for step in (1, 2, 3):
            pl.semaphore_signal(barrier, inc=1, device_id=beside(axis, step), device_id_type=MESH)
    for c in range(32):
        spot = rows_ref[0, 0, c] * 2 + cols_ref[0, 0, c]
        used = jnp.where(counts_ref[0, 0, c] > 0, spot, -1)
        code0[c : c + 1, :] = jnp.full((1, 128), used, jnp.int32).astype(F32)
    get_g.wait()
    gt[...] = g_ref[...].T
    for get in get_x:
        get.wait()
    pl.semaphore_wait(barrier, 10)

    remote(code0, code1, cs, cr, partner)
    sent.append((code0, cs))
    for n in range(4):
        slots = slice(8 * n, 8 * n + 8)
        remote(tiles_ref.at[columns(n), :, other], t1.at[slots], ts.at[n], tr.at[n], partner)
        sent.append((t1.at[slots], ts.at[n]))
    for axis in (X, Y, Z):
        for step in (2, 1, 3):
            remote(xg.at[axis, 3], xg.at[axis, step - 1], gs.at[axis], gr.at[axis], beside(axis, step))
        sent.append((xg.at[axis, 0:3], gs.at[axis]))

    wait(code1, cr)

    def send_x(dx, dy):
        if dx == 2:
            way = dy // 2
            to = beside(X, 1 + 2 * way)
            remote(send[0].at[2, :, dy], ra[0].at[way, :, dy % 2], s1.at[0, 2], ras.at[0, way, 0], to)
        if dx % 2 == 1:
            way = dx // 2

            @pl.when(dy // 2 != way)
            def _():
                block = send[0].at[dx, :, dy]
                remote(block, rb[0].at[way, :, dy], s1.at[0, dx], rps.at[way], beside(X, dx))

    def send_y(dx, dy):
        @pl.when(dy == 2)
        def _():
            for way in range(2):
                pair = slice(2 * way, 2 * way + 2)
                to = beside(Y, 1 + 2 * way)
                remote(send[1].at[2, dx, pair], ra[1].at[way, dx], s1.at[1, 2], ras.at[1, way, dx], to)

        @pl.when(dy % 2 == 1)
        def _():
            way = dy // 2
            pair = pl.ds(2 - 2 * way, 2)
            block = send[1].at[dy, dx, pair]
            remote(block, rb[1].at[way, dx, pair], s1.at[1, dy], rbs.at[1, way, dx], beside(Y, 1 + 2 * way))

    def send_z(dx, dy):
        way = dx // 2
        to = beside(Z, 1 + 2 * way)
        remote(send[2].at[2, dy, dx], ra[2].at[way, dy, dx % 2], s1.at[2, 2], ras.at[2, way, dy], to)
        way = 1 - way
        at1 = 1 + 2 * way
        remote(send[2].at[at1, dy, dx], rb[2].at[way, dy, dx], s1.at[2, at1], rbs.at[2, way, dy], beside(Z, at1))

    def products(n):
        dx = PLACES[n]
        wait(t0.at[8 * n : 8 * n + 8], tl.at[n])
        wait(t1.at[8 * n : 8 * n + 8], tr.at[n])

        def one(i, carry):
            dy = (i + 2) % 4
            for dl in range(2):
                offset = ((pos[1] + dy) % 4) * 2 + (pos[2] + dl) % 2
                c = ((pos[0] + dx) % 4) * 8 + offset
                near = ((pos[2] + dl) % 4) // 2
                own, theirs = t0[8 * n + offset], t1[8 * n + offset]
                code_own = code0[pl.ds(c, 1), :]
                code_theirs = code1[pl.ds(c, 1), :]
                lines = []
                for row in range(2):
                    line = []
                    for col in (near, 1 - near):
                        key = (row * 2 + col).astype(F32)
                        keep_own = jnp.where(code_own == key, 1.0, 0.0).astype(BF16)
                        keep_theirs = jnp.where(code_theirs == key, 1.0, 0.0).astype(BF16)
                        line.append(own * keep_own + theirs * keep_theirs)
                    lines.append(jnp.concatenate(line, axis=1))
                dense = jnp.concatenate(lines, axis=0)
                made = jnp.dot(gt[...], dense, preferred_element_type=F32)
                for part in range(3):
                    rows = slice(FIRST[part], FIRST[part] + ROWS[part])
                    for side in range(2):
                        block = made[rows, side * 128 : (side + 1) * 128]
                        rel = (dx, dy, dl + 2 * side)
                        at = tuple(rel[axis] for axis in ORDERS[part])
                        fixed = at[0] if isinstance(at[0], int) else 1
                        if fixed != 2:
                            full[part][at] = block
                        if fixed != 0:
                            send[part][at] = block.astype(BF16)
            send_x(dx, dy)
            send_y(dx, dy)
            send_z(dx, dy)
            return carry

        lax.fori_loop(0, 4, one, 0)

    def merge1(part, t):
        axis = ORDERS[part][0]
        for way, at1, low in ((0, 1, 0), (1, 3, 2)):
            if part > 0:
                wait(ra[part].at[way, t], ras.at[part, way, t])
            elif t == 2:
                wait(ra[part].at[way], ras.at[part, way, 0])
            for b in range(2):
                send[part][at1, t, low + b] = (full[part][at1, t, low + b] + ra[part][way, t, b].astype(F32)).astype(BF16)
            pair = slice(low, low + 2)
            remote(
                send[part].at[at1, t, pair],
                rb[part].at[way, t, pair],
                s1.at[part, at1],
                rbs.at[part, way, t],
                beside(axis, 1 + 2 * way),
            )

    def sum1(part, t):
        for way in range(2):
            if part > 0:
                wait(rb[part].at[way, t], rbs.at[part, way, t])
            else:
                wait(rb[part].at[way, t, 0:2], rbs.at[part, way, t])
                if t == 2:
                    wait(rb[part].at[way, :, 0:2], rps.at[way])

        def add(b, carry):
            total = full[part][0, t, b] + rb[part][0, t, b].astype(F32) + rb[part][1, t, b].astype(F32)
            full[part][0, t, b] = total
            send[part][0, t, b] = total.astype(BF16)
            return carry

        lax.fori_loop(0, 4, add, 0)

    def step2(part, t):
        axis = ORDERS[part][1]
        sum1(part, t)
        if t > 0:
            remote(send[part].at[0, t], rc[part].at[t - 1], s2.at[part, t - 1], r2.at[part, t - 1], beside(axis, t))

    products(0)
    products(1)
    merge1(1, 2)
    products(2)
    merge1(0, 2)
    merge1(1, 1)
    products(3)
    for part, t in ((2, 2), (0, 1), (1, 3), (2, 1), (0, 3), (2, 3)):
        merge1(part, t)
    for part in (1, 0, 2):
        step2(part, 2)
        merge1(part, 0)
    for t in (1, 3, 0):
        for part in (1, 2, 0):
            step2(part, t)
    for part in range(3):
        for at1 in (1, 2, 3):
            sent.append((send[part].at[at1], s1.at[part, at1]))
        for t in (1, 2, 3):
            sent.append((send[part].at[0, t], s2.at[part, t - 1]))

    def split(value):
        high = value.astype(BF16)
        return high, (value - high.astype(F32)).astype(BF16)

    kept = pl.ds(pl.multiple_of(core * 256, 256), 256)
    given = pl.ds(pl.multiple_of((1 - core) * 256, 256), 256)
    for part in range(3):
        axis = ORDERS[part][2]
        for t in range(3):
            wait(rc[part].at[t], r2.at[part, t])
        for b in range(4):
            near, far, back = (rc[part][t, b].astype(F32) for t in range(3))
            full[part][0, 0, b] = (full[part][0, 0, b] + near) + (far + back)
        wait(xg.at[axis, 0:3], gr.at[axis])
        high, low = split(jnp.concatenate([full[part][0, 0, b] for b in (3, 2, 1, 0)], axis=1))
        owners = xg[axis].reshape(512, 512)
        rows = slice(FIRST[part], FIRST[part] + ROWS[part])
        gw[rows] = jnp.dot(high, owners, preferred_element_type=F32) + jnp.dot(low, owners, preferred_element_type=F32)
        remote(gw.at[rows, given], gwr.at[rows], es.at[part], er.at[part], partner)
        sent.append((gwr.at[rows], es.at[part]))

    def stage3(part):
        axis = ORDERS[part][2]
        for b in (2, 1, 3):
            remote(full[part].at[0, 0, b], rd[part].at[b - 1], s3.at[part, b - 1], r3.at[part, b - 1], beside(axis, b))
            sent.append((rd[part].at[b - 1], s3.at[part, b - 1]))

    def merge_cores(part):
        rows = slice(FIRST[part], FIRST[part] + ROWS[part])
        wait(gwr.at[rows], er.at[part])
        half[rows] = gw[rows, kept] + gwr[rows]

    def scatter(part):
        axis, size = ORDERS[part][0], QUARTER[part]
        for step in (2, 1, 3):
            quarter = pl.ds(pl.multiple_of(QFIRST[part] + ((pos[axis] + step) % 4) * size, 8), size)
            remote(half.at[quarter], x1[part].at[pos[axis]], xs.at[0, part], xr.at[0, part], beside(axis, step))
        x1[part][pos[axis]] = half[pl.ds(pl.multiple_of(QFIRST[part] + pos[axis] * size, 8), size), :]
        sent.append((x1[part].at[0:3], xs.at[0, part]))

    merge_cores(0)
    merge_cores(1)
    scatter(0)
    merge_cores(2)
    scatter(1)
    scatter(2)
    stage3(0)
    for stage, (took, gave) in enumerate(((x1, x2), (x2, x3))):
        for part in range(3):
            axis = ORDERS[part][stage + 1]
            wait(took[part].at[0:3], xr.at[stage, part])
            gave[part][pos[axis]] = (took[part][0] + took[part][1]) + (took[part][2] + took[part][3])
            here = gave[part].at[pos[axis]]
            for step in (2, 1, 3):
                remote(here, here, xs.at[stage + 1, part], xr.at[stage + 1, part], beside(axis, step))
            sent.append((gave[part].at[0:3], xs.at[stage + 1, part]))
        stage3(stage + 1)
    for part in range(3):
        axis, size = ORDERS[part][0], QUARTER[part]
        wait(x3[part].at[0:3], xr.at[2, part])
        rows = pl.ds(pl.multiple_of(QFIRST[part] + pos[axis] * size, 8), size)
        gw_out[rows, kept] = (x3[part][0] + x3[part][1]) + (x3[part][2] + x3[part][3])
        here = gw_out.at[rows, kept]
        for step in (2, 1, 3):
            remote(here, here, xs.at[3, part], xr.at[3, part], beside(axis, step))
        remote(here, here, fs.at[0, part], fr.at[0, part], partner)
        sent.append((x3[part].at[0:3], xs.at[3, part]))
        sent.append((x3[part].at[0], fs.at[0, part]))

    for part in range(3):
        for b in range(3):
            wait(rd[part].at[b], r3.at[part, b])
        rows = slice(FIRST[part], FIRST[part] + ROWS[part])
        tot[rows] = (full[part][0, 0, 0] + rd[part][0]) + (rd[part][1] + rd[part][2])
    high, low = split(tot[...].T)
    get_w.wait()
    last = (((1,), (1,)), ((), ()))
    gf[...] = lax.dot_general(high, w_ref[...], last, preferred_element_type=F32) + lax.dot_general(
        low, w_ref[...], last, preferred_element_type=F32
    )

    for part in range(3):
        axis, size = ORDERS[part][0], QUARTER[part]
        wait(x3[part].at[0:3], xr.at[3, part])
        for step in (1, 2, 3):
            rows = pl.ds(pl.multiple_of(QFIRST[part] + ((pos[axis] + step) % 4) * size, 8), size)
            here = gw_out.at[rows, kept]
            remote(here, here, fs.at[1, part], fr.at[1, part], partner)
        sent.append((x3[part].at[0:3], fs.at[1, part]))
    for part in range(3):
        wait(x3[part].at[0], fr.at[0, part])
        wait(x3[part].at[0:3], fr.at[1, part])
    finish()


def body(tile_values, tile_rows, tile_cols, tile_counts, grad_out, features, weight):
    tiles = tile_values[0, 0, :, 0]
    anywhere = pl.BlockSpec(memory_space=pl.ANY)
    smem = pl.BlockSpec(memory_space=pltpu.SMEM)

    def per_part(*shape, dtype, rows=ROWS, lanes=128):
        return [pltpu.VMEM((*shape, r, lanes), dtype) for r in rows]

    dma = pltpu.SemaphoreType.DMA
    scratch = [
        pltpu.VMEM((32, 256, 128), BF16),
        pltpu.VMEM((32, 256, 128), BF16),
        pltpu.VMEM((32, 128), F32),
        pltpu.VMEM((32, 128), F32),
        pltpu.VMEM((512, 512), BF16),
        pltpu.VMEM((512, 512), BF16),
        pltpu.VMEM((512, 512), BF16),
        pltpu.VMEM((3, 4, 128, 512), BF16),
        *per_part(4, 4, 4, dtype=BF16),
        *per_part(4, 4, 4, dtype=F32),
        *per_part(2, 4, 2, dtype=BF16),
        *per_part(2, 4, 4, dtype=BF16),
        *per_part(3, 4, dtype=BF16),
        *per_part(3, dtype=F32),
        pltpu.VMEM((512, 128), F32),
        pltpu.VMEM((512, 512), F32),
        pltpu.VMEM((512, 256), F32),
        pltpu.VMEM((512, 256), F32),
    ]
    for _ in range(3):
        scratch += per_part(4, dtype=F32, rows=QUARTER, lanes=256)
    scratch += [
        dma((5,)),
        dma((3,)),
        dma((3,)),
        dma((4,)),
        dma((4,)),
        dma((4,)),
        dma,
        dma,
        dma((3, 4)),
        dma((3, 2, 4)),
        dma((3, 2, 4)),
        dma((2,)),
        dma((3, 3)),
        dma((3, 3)),
        dma((3, 3)),
        dma((3, 3)),
        dma((3,)),
        dma((3,)),
        dma((4, 3)),
        dma((4, 3)),
        dma((2, 3)),
        dma((2, 3)),
    ]
    vmem = pl.BlockSpec(memory_space=pltpu.VMEM)
    grad_features, turned = pl.pallas_call(
        kernel,
        out_shape=(pltpu.VMEM((128, 512), F32), pltpu.VMEM((512, 512), F32)),
        in_specs=[smem, smem, smem, anywhere, anywhere, anywhere, anywhere],
        out_specs=(vmem, vmem),
        scratch_shapes=scratch,
        compiler_params=pltpu.CompilerParams(
            collective_id=0, has_side_effects=True, vmem_limit_bytes=56 * 1024 * 1024
        ),
    )(tile_rows[..., 0], tile_cols[..., 0], tile_counts, tiles, grad_out, features, weight)
    return grad_features, turned.T


def solution(mesh):
    placed = (
        P("blk", "rep", None, None, None, None),
        P("blk", "rep", None, None),
        P("blk", "rep", None, None),
        P("blk", "rep", None),
        P("blk", None),
        P(("blk", "rep"), None),
        P(),
    )
    return jax.shard_map(
        body, mesh=mesh, in_specs=placed, out_specs=(P(("blk", "rep"), None), P()), check_vma=False
    )
```

time: 77.3 us -> 74.5 us (0.964)
  Pallas kernels: 74.5 us -> 71.7 us
    pallas_call x1, Pallas kernels: 74.5 us -> 71.7 us  [body(): pl.pallas_call(kernel, out_shape=(pltpu.VMEM((128, 512), F32), pltpu.VMEM...]
where the time goes in v4:
time: 74.5 us; the launch traced here: 74.4 us
  Pallas kernels  71.7 us (96%)
  local copies, waits for them, and re-layouts  2.01 us (3%)
    pallas_call x1, Pallas kernels, body(): pl.pallas_call(kernel, out_shape=(pltpu.VMEM((128, 512), F32), pltpu.VMEM...  71.7 us
    unnamed x2, local copies, waits for them, and re-layouts  2.01 us

profile of v4, /device:TPU:1, one launch (start us, length us, event | category | flops | bytes accessed | tf_op | source)
XLA Modules:
  0.0 74.4 jit_solution(14988015742497834078)
XLA Ops:
  0.6 71.7 %shard_map.86 = (f32[128,512]{1,0:T(8,128)S(1)}, f32[512,512]{1,0:T(8,128)S(1)}) custom-call(s32[1,1,32]{2,1,0:T(1,128)} %bitcast.6, s32[1,1,32]{2,1,0:T(1,128)} %bitcast.7, s32[1,1,32]{2,1,0:T(1,128)} %counts_ref.1, bf16[32,256,256]{2,1,0:T(8,128)(2,1)} %bitcast.5, bf16[512,512]{1,0:T(8,128)(2,1)} %g_any.1, bf16[128,512]{1,0:T(8,128)(2,1)} %x_any.1, ...), custom_call_target="tpu_custom_call" | custom-call | tf_op jit(solution)/shard_map/pallas_call | solution.py:399
  72.3 0.7 copy.11
  73.0 1.3 %copy.9 = f32[512,512]{1,0:T(8,128)} copy(f32[512,512]{0,1:T(8,128)S(1)} %bitcast.4) | data formatting | bytes 2097152

commit v5 on v4

--- a/solution.py
+++ b/solution.py
@@ -24,10 +24,10 @@
     (t0, t1, code0, code1, g_ref, w_ref, gt, xg, *rest) = scratch
     send = rest[0:3]
     full = rest[3:6]
-    ra, rb, rc, rd = rest[6:9], rest[9:12], rest[12:15], rest[15:18]
-    tot, gw, gwr, half = rest[18:22]
-    x1, x2, x3 = rest[22:25], rest[25:28], rest[28:31]
-    (ins, gs, gr, tl, ts, tr, cs, cr, s1, ras, rbs, rps, s2, r2, s3, r3, es, er, xs, xr, fs, fr) = rest[31:]
+    ra, rb, r2a, rc, rd = rest[6:9], rest[9:12], rest[12:15], rest[15:18], rest[18:21]
+    tot, gw, gwr, half = rest[21:25]
+    x1, x2, x3 = rest[25:28], rest[28:31], rest[31:34]
+    (ins, gs, gr, tl, ts, tr, cs, cr, s1, ras, rbs, rps, s2, r2, s3, r3, es, er, xs, xr, fs, fr) = rest[34:]
 
     blk = lax.axis_index("blk")
     rep = lax.axis_index("rep")
@@ -55,11 +55,14 @@
     mine = pl.ds(pl.multiple_of(core * 128, 128), 128)
     other = pl.ds(pl.multiple_of((1 - core) * 128, 128), 128)
 
+    barrier = pltpu.get_barrier_semaphore()
+    for axis in (X, Y, Z):
+        for step in (2, 1, 3):
+            pl.semaphore_signal(barrier, inc=1, device_id=beside(axis, step), device_id_type=MESH)
+    pl.semaphore_signal(barrier, inc=1, device_id=partner, device_id_type=MESH)
+
     def columns(n):
         return pl.ds(((pos[0] + PLACES[n]) % 4) * 8, 8)
-
-    for n in range(4):
-        pltpu.make_async_copy(tiles_ref.at[columns(n), :, mine], t0.at[8 * n : 8 * n + 8], tl.at[n]).start()
 
     def fetch(src, dst, sem):
         copy = pltpu.make_async_copy(src, dst, sem)
@@ -67,6 +70,8 @@
         return copy
 
     get_g = fetch(g_any, g_ref, ins.at[0])
+    for n in range(4):
+        fetch(tiles_ref.at[columns(n), :, mine], t0.at[8 * n : 8 * n + 8], tl.at[n])
     get_x = [fetch(x_any, xg.at[axis, 3], ins.at[1 + axis]) for axis in (X, Y, Z)]
     get_w = fetch(w_any, w_ref, ins.at[4])
 
@@ -76,32 +81,30 @@
         for region, sem in sent:
             wait(region, sem)
 
-    barrier = pltpu.get_barrier_semaphore()
-    pl.semaphore_signal(barrier, inc=1, device_id=partner, device_id_type=MESH)
-    for axis in (X, Y, Z):
-        for step in (1, 2, 3):
-            pl.semaphore_signal(barrier, inc=1, device_id=beside(axis, step), device_id_type=MESH)
     for c in range(32):
         spot = rows_ref[0, 0, c] * 2 + cols_ref[0, 0, c]
         used = jnp.where(counts_ref[0, 0, c] > 0, spot, -1)
         code0[c : c + 1, :] = jnp.full((1, 128), used, jnp.int32).astype(F32)
+    pl.semaphore_wait(barrier, 10)
+
+    def swap(n):
+        slots = slice(8 * n, 8 * n + 8)
+        remote(tiles_ref.at[columns(n), :, other], t1.at[slots], ts.at[n], tr.at[n], partner)
+        sent.append((t1.at[slots], ts.at[n]))
+
+    remote(code0, code1, cs, cr, partner)
+    sent.append((code0, cs))
+    swap(0)
+    for axis in (X, Y, Z):
+        for step in (2, 1, 3):
+            remote(x_any, xg.at[axis, step - 1], gs.at[axis], gr.at[axis], beside(axis, step))
+        sent.append((xg.at[axis, 0:3], gs.at[axis]))
+    for n in range(1, 4):
+        swap(n)
     get_g.wait()
     gt[...] = g_ref[...].T
     for get in get_x:
         get.wait()
-    pl.semaphore_wait(barrier, 10)
-
-    remote(code0, code1, cs, cr, partner)
-    sent.append((code0, cs))
-    for n in range(4):
-        slots = slice(8 * n, 8 * n + 8)
-        remote(tiles_ref.at[columns(n), :, other], t1.at[slots], ts.at[n], tr.at[n], partner)
-        sent.append((t1.at[slots], ts.at[n]))
-    for axis in (X, Y, Z):
-        for step in (2, 1, 3):
-            remote(xg.at[axis, 3], xg.at[axis, step - 1], gs.at[axis], gr.at[axis], beside(axis, step))
-        sent.append((xg.at[axis, 0:3], gs.at[axis]))
-
     wait(code1, cr)
 
     def send_x(dx, dy):
@@ -222,7 +225,26 @@
         axis = ORDERS[part][1]
         sum1(part, t)
         if t > 0:
-            remote(send[part].at[0, t], rc[part].at[t - 1], s2.at[part, t - 1], r2.at[part, t - 1], beside(axis, t))
+            source = send[part].at[0, t]
+        if t == 2:
+            for way in range(2):
+                pair = source.at[2 * way : 2 * way + 2]
+                remote(pair, r2a[part].at[way], s2.at[part, 0], r2.at[part, way], beside(axis, 1 + 2 * way))
+        elif t > 0:
+            way = t // 2
+            pair = slice(2 - 2 * way, 4 - 2 * way)
+            remote(source.at[pair], rc[part].at[way, pair], s2.at[part, t], r2.at[part, 2 + way], beside(axis, t))
+
+    def merge2(part):
+        axis = ORDERS[part][1]
+        for way, t in ((0, 1), (1, 3)):
+            wait(r2a[part].at[way], r2.at[part, way])
+            for b in range(2):
+                at = (0, t, 2 * way + b)
+                send[part][at] = (full[part][at] + r2a[part][way, b].astype(F32)).astype(BF16)
+            pair = slice(2 * way, 2 * way + 2)
+            source = send[part].at[0, t, pair]
+            remote(source, rc[part].at[way, pair], s2.at[part, t], r2.at[part, 2 + way], beside(axis, t))
 
     products(0)
     products(1)
@@ -236,14 +258,18 @@
     for part in (1, 0, 2):
         step2(part, 2)
         merge1(part, 0)
-    for t in (1, 3, 0):
-        for part in (1, 2, 0):
+    for t in (1, 3):
+        for part in (1, 0, 2):
             step2(part, t)
+            if t == 3:
+                merge2(part)
+    for part in (1, 0, 2):
+        step2(part, 0)
     for part in range(3):
         for at1 in (1, 2, 3):
             sent.append((send[part].at[at1], s1.at[part, at1]))
-        for t in (1, 2, 3):
-            sent.append((send[part].at[0, t], s2.at[part, t - 1]))
+        for t, sem in ((1, 1), (2, 0), (3, 3)):
+            sent.append((send[part].at[0, t], s2.at[part, sem]))
 
     def split(value):
         high = value.astype(BF16)
@@ -253,11 +279,11 @@
     given = pl.ds(pl.multiple_of((1 - core) * 256, 256), 256)
     for part in range(3):
         axis = ORDERS[part][2]
-        for t in range(3):
-            wait(rc[part].at[t], r2.at[part, t])
+        for way in range(2):
+            wait(rc[part].at[way], r2.at[part, 2 + way])
         for b in range(4):
-            near, far, back = (rc[part][t, b].astype(F32) for t in range(3))
-            full[part][0, 0, b] = (full[part][0, 0, b] + near) + (far + back)
+            near, back = (rc[part][way, b].astype(F32) for way in range(2))
+            full[part][0, 0, b] = full[part][0, 0, b] + (near + back)
         wait(xg.at[axis, 0:3], gr.at[axis])
         high, low = split(jnp.concatenate([full[part][0, 0, b] for b in (3, 2, 1, 0)], axis=1))
         owners = xg[axis].reshape(512, 512)
@@ -266,11 +292,12 @@
         remote(gw.at[rows, given], gwr.at[rows], es.at[part], er.at[part], partner)
         sent.append((gwr.at[rows], es.at[part]))
 
-    def stage3(part):
-        axis = ORDERS[part][2]
-        for b in (2, 1, 3):
-            remote(full[part].at[0, 0, b], rd[part].at[b - 1], s3.at[part, b - 1], r3.at[part, b - 1], beside(axis, b))
-            sent.append((rd[part].at[b - 1], s3.at[part, b - 1]))
+    def stage3(*places):
+        for part in range(3):
+            axis = ORDERS[part][2]
+            for b in places:
+                remote(full[part].at[0, 0, b], rd[part].at[b - 1], s3.at[part, b - 1], r3.at[part, b - 1], beside(axis, b))
+                sent.append((rd[part].at[b - 1], s3.at[part, b - 1]))
 
     def merge_cores(part):
         rows = slice(FIRST[part], FIRST[part] + ROWS[part])
@@ -291,7 +318,7 @@
     merge_cores(2)
     scatter(1)
     scatter(2)
-    stage3(0)
+    stage3(2)
     for stage, (took, gave) in enumerate(((x1, x2), (x2, x3))):
         for part in range(3):
             axis = ORDERS[part][stage + 1]
@@ -301,7 +328,10 @@
             for step in (2, 1, 3):
                 remote(here, here, xs.at[stage + 1, part], xr.at[stage + 1, part], beside(axis, step))
             sent.append((gave[part].at[0:3], xs.at[stage + 1, part]))
-        stage3(stage + 1)
+        if stage == 0:
+            stage3(1, 3)
+    early = list(sent)
+    sent.clear()
     for part in range(3):
         axis, size = ORDERS[part][0], QUARTER[part]
         wait(x3[part].at[0:3], xr.at[2, part])
@@ -325,6 +355,9 @@
     gf[...] = lax.dot_general(high, w_ref[...], last, preferred_element_type=F32) + lax.dot_general(
         low, w_ref[...], last, preferred_element_type=F32
     )
+
+    for region, sem in early:
+        wait(region, sem)
 
     for part in range(3):
         axis, size = ORDERS[part][0], QUARTER[part]
@@ -362,7 +395,8 @@
         *per_part(4, 4, 4, dtype=F32),
         *per_part(2, 4, 2, dtype=BF16),
         *per_part(2, 4, 4, dtype=BF16),
-        *per_part(3, 4, dtype=BF16),
+        *per_part(2, 2, dtype=BF16),
+        *per_part(2, 4, dtype=BF16),
         *per_part(3, dtype=F32),
         pltpu.VMEM((512, 128), F32),
         pltpu.VMEM((512, 512), F32),
@@ -384,8 +418,8 @@
         dma((3, 2, 4)),
         dma((3, 2, 4)),
         dma((2,)),
-        dma((3, 3)),
-        dma((3, 3)),
+        dma((3, 4)),
+        dma((3, 4)),
         dma((3, 3)),
         dma((3, 3)),
         dma((3,)),

time: 74.5 us -> 71.5 us (0.960)
  Pallas kernels: 71.7 us -> 68.7 us
    pallas_call x1, Pallas kernels: 71.7 us -> 68.7 us  [body(): pl.pallas_call(kernel, out_shape=(pltpu.VMEM((128, 512), F32), pltpu.VMEM...]
where the time goes in v5:
time: 71.5 us; the launch traced here: 71.4 us
  Pallas kernels  68.7 us (96%)
  local copies, waits for them, and re-layouts  2.01 us (3%)
    pallas_call x1, Pallas kernels, body(): pl.pallas_call(kernel, out_shape=(pltpu.VMEM((128, 512), F32), pltpu.VMEM...  68.7 us
    unnamed x2, local copies, waits for them, and re-layouts  2.01 us

profile of v5, /device:TPU:1, one launch (start us, length us, event | category | flops | bytes accessed | tf_op | source)
XLA Modules:
  0.0 71.4 jit_solution(165881745272674767)
XLA Ops:
  0.6 68.7 %shard_map.86 = (f32[128,512]{1,0:T(8,128)S(1)}, f32[512,512]{1,0:T(8,128)S(1)}) custom-call(s32[1,1,32]{2,1,0:T(1,128)} %bitcast.6, s32[1,1,32]{2,1,0:T(1,128)} %bitcast.7, s32[1,1,32]{2,1,0:T(1,128)} %counts_ref.1, bf16[32,256,256]{2,1,0:T(8,128)(2,1)} %bitcast.5, bf16[512,512]{1,0:T(8,128)(2,1)} %g_any.1, bf16[128,512]{1,0:T(8,128)(2,1)} %x_any.1, ...), custom_call_target="tpu_custom_call" | custom-call | tf_op jit(solution)/shard_map/pallas_call | solution.py:433
  69.4 0.7 copy.11
  70.1 1.3 %copy.9 = f32[512,512]{1,0:T(8,128)} copy(f32[512,512]{0,1:T(8,128)S(1)} %bitcast.4) | data formatting | bytes 2097152

commit v6 on v5

--- a/solution.py
+++ b/solution.py
@@ -15,8 +15,8 @@
 FIRST = (0, 176, 352)
 X, Y, Z = 0, 1, 2
 ORDERS = ((X, Z, Y), (Y, X, Z), (Z, Y, X))
-QUARTER = (48, 48, 32)
-QFIRST = (0, 192, 384)
+QUARTER = (24, 24, 16, 24, 24, 16)
+QFIRST = (0, 96, 192, 256, 352, 448)
 PLACES = (2, 1, 3, 0)
 
 
@@ -26,8 +26,8 @@
     full = rest[3:6]
     ra, rb, r2a, rc, rd = rest[6:9], rest[9:12], rest[12:15], rest[15:18], rest[18:21]
     tot, gw, gwr, half = rest[21:25]
-    x1, x2, x3 = rest[25:28], rest[28:31], rest[31:34]
-    (ins, gs, gr, tl, ts, tr, cs, cr, s1, ras, rbs, rps, s2, r2, s3, r3, es, er, xs, xr, fs, fr) = rest[34:]
+    x1, x2, x3 = rest[25:31], rest[31:37], rest[37:43]
+    (ins, gs, gr, tl, ts, tr, cs, cr, s1, ras, rbs, rps, s2, r2, s3, r3, es, er, xs, xr, fs, fr) = rest[43:]
 
     blk = lax.axis_index("blk")
     rep = lax.axis_index("rep")
@@ -250,10 +250,8 @@
     products(1)
     merge1(1, 2)
     products(2)
-    merge1(0, 2)
-    merge1(1, 1)
     products(3)
-    for part, t in ((2, 2), (0, 1), (1, 3), (2, 1), (0, 3), (2, 3)):
+    for part, t in ((1, 1), (0, 2), (2, 2), (0, 1), (1, 3), (2, 1), (0, 3), (2, 3)):
         merge1(part, t)
     for part in (1, 0, 2):
         step2(part, 2)
@@ -271,6 +269,12 @@
         for t, sem in ((1, 1), (2, 0), (3, 3)):
             sent.append((send[part].at[0, t], s2.at[part, sem]))
 
+    def stage3(part, *places):
+        axis = ORDERS[part][2]
+        for b in places:
+            remote(full[part].at[0, 0, b], rd[part].at[b - 1], s3.at[part, b - 1], r3.at[part, b - 1], beside(axis, b))
+            sent.append((rd[part].at[b - 1], s3.at[part, b - 1]))
+
     def split(value):
         high = value.astype(BF16)
         return high, (value - high.astype(F32)).astype(BF16)
@@ -284,6 +288,7 @@
         for b in range(4):
             near, back = (rc[part][way, b].astype(F32) for way in range(2))
             full[part][0, 0, b] = full[part][0, 0, b] + (near + back)
+        stage3(part, 2)
         wait(xg.at[axis, 0:3], gr.at[axis])
         high, low = split(jnp.concatenate([full[part][0, 0, b] for b in (3, 2, 1, 0)], axis=1))
         owners = xg[axis].reshape(512, 512)
@@ -292,57 +297,51 @@
         remote(gw.at[rows, given], gwr.at[rows], es.at[part], er.at[part], partner)
         sent.append((gwr.at[rows], es.at[part]))
 
-    def stage3(*places):
-        for part in range(3):
-            axis = ORDERS[part][2]
-            for b in places:
-                remote(full[part].at[0, 0, b], rd[part].at[b - 1], s3.at[part, b - 1], r3.at[part, b - 1], beside(axis, b))
-                sent.append((rd[part].at[b - 1], s3.at[part, b - 1]))
-
     def merge_cores(part):
         rows = slice(FIRST[part], FIRST[part] + ROWS[part])
         wait(gwr.at[rows], er.at[part])
         half[rows] = gw[rows, kept] + gwr[rows]
 
-    def scatter(part):
-        axis, size = ORDERS[part][0], QUARTER[part]
+    def scatter(piece):
+        axis, size = ORDERS[piece % 3][0], QUARTER[piece]
         for step in (2, 1, 3):
-            quarter = pl.ds(pl.multiple_of(QFIRST[part] + ((pos[axis] + step) % 4) * size, 8), size)
-            remote(half.at[quarter], x1[part].at[pos[axis]], xs.at[0, part], xr.at[0, part], beside(axis, step))
-        x1[part][pos[axis]] = half[pl.ds(pl.multiple_of(QFIRST[part] + pos[axis] * size, 8), size), :]
-        sent.append((x1[part].at[0:3], xs.at[0, part]))
+            quarter = pl.ds(pl.multiple_of(QFIRST[piece] + ((pos[axis] + step) % 4) * size, 8), size)
+            remote(half.at[quarter], x1[piece].at[pos[axis]], xs.at[0, piece], xr.at[0, piece], beside(axis, step))
+        x1[piece][pos[axis]] = half[pl.ds(pl.multiple_of(QFIRST[piece] + pos[axis] * size, 8), size), :]
+        sent.append((x1[piece].at[0:3], xs.at[0, piece]))
 
     merge_cores(0)
+    scatter(0)
     merge_cores(1)
-    scatter(0)
-    merge_cores(2)
     scatter(1)
     scatter(2)
-    stage3(2)
+    merge_cores(2)
+    for piece in range(3, 6):
+        scatter(piece)
+    for part in range(3):
+        stage3(part, 1, 3)
     for stage, (took, gave) in enumerate(((x1, x2), (x2, x3))):
-        for part in range(3):
-            axis = ORDERS[part][stage + 1]
-            wait(took[part].at[0:3], xr.at[stage, part])
-            gave[part][pos[axis]] = (took[part][0] + took[part][1]) + (took[part][2] + took[part][3])
-            here = gave[part].at[pos[axis]]
+        for piece in range(6):
+            axis = ORDERS[piece % 3][stage + 1]
+            wait(took[piece].at[0:3], xr.at[stage, piece])
+            gave[piece][pos[axis]] = (took[piece][0] + took[piece][1]) + (took[piece][2] + took[piece][3])
+            here = gave[piece].at[pos[axis]]
             for step in (2, 1, 3):
-                remote(here, here, xs.at[stage + 1, part], xr.at[stage + 1, part], beside(axis, step))
-            sent.append((gave[part].at[0:3], xs.at[stage + 1, part]))
-        if stage == 0:
-            stage3(1, 3)
+                remote(here, here, xs.at[stage + 1, piece], xr.at[stage + 1, piece], beside(axis, step))
+            sent.append((gave[piece].at[0:3], xs.at[stage + 1, piece]))
     early = list(sent)
     sent.clear()
-    for part in range(3):
-        axis, size = ORDERS[part][0], QUARTER[part]
-        wait(x3[part].at[0:3], xr.at[2, part])
-        rows = pl.ds(pl.multiple_of(QFIRST[part] + pos[axis] * size, 8), size)
-        gw_out[rows, kept] = (x3[part][0] + x3[part][1]) + (x3[part][2] + x3[part][3])
+    for piece in range(6):
+        axis, size = ORDERS[piece % 3][0], QUARTER[piece]
+        wait(x3[piece].at[0:3], xr.at[2, piece])
+        rows = pl.ds(pl.multiple_of(QFIRST[piece] + pos[axis] * size, 8), size)
+        gw_out[rows, kept] = (x3[piece][0] + x3[piece][1]) + (x3[piece][2] + x3[piece][3])
         here = gw_out.at[rows, kept]
         for step in (2, 1, 3):
-            remote(here, here, xs.at[3, part], xr.at[3, part], beside(axis, step))
-        remote(here, here, fs.at[0, part], fr.at[0, part], partner)
-        sent.append((x3[part].at[0:3], xs.at[3, part]))
-        sent.append((x3[part].at[0], fs.at[0, part]))
+            remote(here, here, xs.at[3, piece], xr.at[3, piece], beside(axis, step))
+        remote(here, here, fs.at[0, piece], fr.at[0, piece], partner)
+        sent.append((x3[piece].at[0:3], xs.at[3, piece]))
+        sent.append((x3[piece].at[0], fs.at[0, piece]))
 
     for part in range(3):
         for b in range(3):
@@ -359,17 +358,17 @@
     for region, sem in early:
         wait(region, sem)
 
-    for part in range(3):
-        axis, size = ORDERS[part][0], QUARTER[part]
-        wait(x3[part].at[0:3], xr.at[3, part])
+    for piece in range(6):
+        axis, size = ORDERS[piece % 3][0], QUARTER[piece]
+        wait(x3[piece].at[0:3], xr.at[3, piece])
         for step in (1, 2, 3):
-            rows = pl.ds(pl.multiple_of(QFIRST[part] + ((pos[axis] + step) % 4) * size, 8), size)
+            rows = pl.ds(pl.multiple_of(QFIRST[piece] + ((pos[axis] + step) % 4) * size, 8), size)
             here = gw_out.at[rows, kept]
-            remote(here, here, fs.at[1, part], fr.at[1, part], partner)
-        sent.append((x3[part].at[0:3], fs.at[1, part]))
-    for part in range(3):
-        wait(x3[part].at[0], fr.at[0, part])
-        wait(x3[part].at[0:3], fr.at[1, part])
+            remote(here, here, fs.at[1, piece], fr.at[1, piece], partner)
+        sent.append((x3[piece].at[0:3], fs.at[1, piece]))
+    for piece in range(6):
+        wait(x3[piece].at[0], fr.at[0, piece])
+        wait(x3[piece].at[0:3], fr.at[1, piece])
     finish()
 
 
@@ -424,10 +423,10 @@
         dma((3, 3)),
         dma((3,)),
         dma((3,)),
-        dma((4, 3)),
-        dma((4, 3)),
-        dma((2, 3)),
-        dma((2, 3)),
+        dma((4, 6)),
+        dma((4, 6)),
+        dma((2, 6)),
+        dma((2, 6)),
     ]
     vmem = pl.BlockSpec(memory_space=pltpu.VMEM)
     grad_features, turned = pl.pallas_call(

time: 71.5 us -> 70.3 us (0.983)
  Pallas kernels: 68.7 us -> 67.5 us
    pallas_call x1, Pallas kernels: 68.7 us -> 67.5 us  [body(): pl.pallas_call(kernel, out_shape=(pltpu.VMEM((128, 512), F32), pltpu.VMEM...]
where the time goes in v6:
time: 70.3 us; the launch traced here: 70.2 us
  Pallas kernels  67.5 us (96%)
  local copies, waits for them, and re-layouts  2.01 us (3%)
    pallas_call x1, Pallas kernels, body(): pl.pallas_call(kernel, out_shape=(pltpu.VMEM((128, 512), F32), pltpu.VMEM...  67.5 us
    unnamed x2, local copies, waits for them, and re-layouts  2.01 us

profile of v6, /device:TPU:1, one launch (start us, length us, event | category | flops | bytes accessed | tf_op | source)
XLA Modules:
  0.0 70.2 jit_solution(210491886200328588)
XLA Ops:
  0.6 67.5 %shard_map.86 = (f32[128,512]{1,0:T(8,128)S(1)}, f32[512,512]{1,0:T(8,128)S(1)}) custom-call(s32[1,1,32]{2,1,0:T(1,128)} %bitcast.6, s32[1,1,32]{2,1,0:T(1,128)} %bitcast.7, s32[1,1,32]{2,1,0:T(1,128)} %counts_ref.1, bf16[32,256,256]{2,1,0:T(8,128)(2,1)} %bitcast.5, bf16[512,512]{1,0:T(8,128)(2,1)} %g_any.1, bf16[128,512]{1,0:T(8,128)(2,1)} %x_any.1, ...), custom_call_target="tpu_custom_call" | custom-call | tf_op jit(solution)/shard_map/pallas_call | solution.py:432
  68.2 0.7 %copy.11 = f32[128,512]{1,0:T(8,128)} copy(f32[128,512]{1,0:T(8,128)S(1)} %get-tuple-element.8) | data formatting | bytes 524288
  68.9 1.3 %copy.9 = f32[512,512]{1,0:T(8,128)} copy(f32[512,512]{0,1:T(8,128)S(1)} %bitcast.4) | data formatting | bytes 2097152

commit v7 on v6

--- a/solution.py
+++ b/solution.py
@@ -15,8 +15,8 @@
 FIRST = (0, 176, 352)
 X, Y, Z = 0, 1, 2
 ORDERS = ((X, Z, Y), (Y, X, Z), (Z, Y, X))
-QUARTER = (24, 24, 16, 24, 24, 16)
-QFIRST = (0, 96, 192, 256, 352, 448)
+QUARTER = (16, 16, 16, 16, 16, 16, 16, 8, 8)
+QFIRST = (0, 64, 128, 192, 256, 320, 384, 448, 480)
 PLACES = (2, 1, 3, 0)
 
 
@@ -26,8 +26,8 @@
     full = rest[3:6]
     ra, rb, r2a, rc, rd = rest[6:9], rest[9:12], rest[12:15], rest[15:18], rest[18:21]
     tot, gw, gwr, half = rest[21:25]
-    x1, x2, x3 = rest[25:31], rest[31:37], rest[37:43]
-    (ins, gs, gr, tl, ts, tr, cs, cr, s1, ras, rbs, rps, s2, r2, s3, r3, es, er, xs, xr, fs, fr) = rest[43:]
+    x1, x2, x3 = rest[25:34], rest[34:43], rest[43:52]
+    (ins, gs, gr, tl, ts, tr, cs, cr, s1, ras, rbs, rps, s2, r2, s3, r3, es, er, xs, xr, fs, fr) = rest[52:]
 
     blk = lax.axis_index("blk")
     rep = lax.axis_index("rep")
@@ -251,7 +251,7 @@
     merge1(1, 2)
     products(2)
     products(3)
-    for part, t in ((1, 1), (0, 2), (2, 2), (0, 1), (1, 3), (2, 1), (0, 3), (2, 3)):
+    for part, t in ((1, 1), (0, 2), (1, 3), (0, 1), (2, 2), (0, 3), (2, 1), (2, 3)):
         merge1(part, t)
     for part in (1, 0, 2):
         step2(part, 2)
@@ -281,7 +281,7 @@
 
     kept = pl.ds(pl.multiple_of(core * 256, 256), 256)
     given = pl.ds(pl.multiple_of((1 - core) * 256, 256), 256)
-    for part in range(3):
+    for part in (1, 0, 2):
         axis = ORDERS[part][2]
         for way in range(2):
             wait(rc[part].at[way], r2.at[part, 2 + way])
@@ -312,16 +312,18 @@
 
     merge_cores(0)
     scatter(0)
+    scatter(1)
     merge_cores(1)
-    scatter(1)
     scatter(2)
+    scatter(3)
+    scatter(4)
     merge_cores(2)
-    for piece in range(3, 6):
+    for piece in range(5, 9):
         scatter(piece)
     for part in range(3):
         stage3(part, 1, 3)
     for stage, (took, gave) in enumerate(((x1, x2), (x2, x3))):
-        for piece in range(6):
+        for piece in range(9):
             axis = ORDERS[piece % 3][stage + 1]
             wait(took[piece].at[0:3], xr.at[stage, piece])
             gave[piece][pos[axis]] = (took[piece][0] + took[piece][1]) + (took[piece][2] + took[piece][3])
@@ -331,7 +333,7 @@
             sent.append((gave[piece].at[0:3], xs.at[stage + 1, piece]))
     early = list(sent)
     sent.clear()
-    for piece in range(6):
+    for piece in range(9):
         axis, size = ORDERS[piece % 3][0], QUARTER[piece]
         wait(x3[piece].at[0:3], xr.at[2, piece])
         rows = pl.ds(pl.multiple_of(QFIRST[piece] + pos[axis] * size, 8), size)
@@ -358,7 +360,7 @@
     for region, sem in early:
         wait(region, sem)
 
-    for piece in range(6):
+    for piece in range(9):
         axis, size = ORDERS[piece % 3][0], QUARTER[piece]
         wait(x3[piece].at[0:3], xr.at[3, piece])
         for step in (1, 2, 3):
@@ -366,7 +368,7 @@
             here = gw_out.at[rows, kept]
             remote(here, here, fs.at[1, piece], fr.at[1, piece], partner)
         sent.append((x3[piece].at[0:3], fs.at[1, piece]))
-    for piece in range(6):
+    for piece in range(9):
         wait(x3[piece].at[0], fr.at[0, piece])
         wait(x3[piece].at[0:3], fr.at[1, piece])
     finish()
@@ -423,10 +425,10 @@
         dma((3, 3)),
         dma((3,)),
         dma((3,)),
-        dma((4, 6)),
-        dma((4, 6)),
-        dma((2, 6)),
-        dma((2, 6)),
+        dma((4, 9)),
+        dma((4, 9)),
+        dma((2, 9)),
+        dma((2, 9)),
     ]
     vmem = pl.BlockSpec(memory_space=pltpu.VMEM)
     grad_features, turned = pl.pallas_call(

time: 70.3 us -> 69.4 us (0.987)
  Pallas kernels: 67.5 us -> 66.7 us
    pallas_call x1, Pallas kernels: 67.5 us -> 66.7 us  [body(): pl.pallas_call(kernel, out_shape=(pltpu.VMEM((128, 512), F32), pltpu.VMEM...]
where the time goes in v7:
time: 69.4 us; the launch traced here: 69.3 us
  Pallas kernels  66.7 us (96%)
  local copies, waits for them, and re-layouts  2.01 us (3%)
    pallas_call x1, Pallas kernels, body(): pl.pallas_call(kernel, out_shape=(pltpu.VMEM((128, 512), F32), pltpu.VMEM...  66.7 us
    unnamed x2, local copies, waits for them, and re-layouts  2.01 us

profile of v7, /device:TPU:1, one launch (start us, length us, event | category | flops | bytes accessed | tf_op | source)
XLA Modules:
  0.0 69.3 jit_solution(9255262866092496803)
XLA Ops:
  0.6 66.7 %shard_map.86 = (f32[128,512]{1,0:T(8,128)S(1)}, f32[512,512]{1,0:T(8,128)S(1)}) custom-call(s32[1,1,32]{2,1,0:T(1,128)} %bitcast.6, s32[1,1,32]{2,1,0:T(1,128)} %bitcast.7, s32[1,1,32]{2,1,0:T(1,128)} %counts_ref.1, bf16[32,256,256]{2,1,0:T(8,128)(2,1)} %bitcast.5, bf16[512,512]{1,0:T(8,128)(2,1)} %g_any.1, bf16[128,512]{1,0:T(8,128)(2,1)} %x_any.1, ...), custom_call_target="tpu_custom_call" | custom-call | tf_op jit(solution)/shard_map/pallas_call | solution.py:434
  67.3 0.7 %copy.11 = f32[128,512]{1,0:T(8,128)} copy(f32[128,512]{1,0:T(8,128)S(1)} %get-tuple-element.8) | data formatting | bytes 524288
  68.0 1.3 %copy.9 = f32[512,512]{1,0:T(8,128)} copy(f32[512,512]{0,1:T(8,128)S(1)} %bitcast.4) | data formatting | bytes 2097152

commit v8 on v7

--- a/solution.py
+++ b/solution.py
@@ -149,7 +149,7 @@
         wait(t1.at[8 * n : 8 * n + 8], tr.at[n])
 
         def one(i, carry):
-            dy = (i + 2) % 4
+            dy = (2 + 3 * i) % 4
             for dl in range(2):
                 offset = ((pos[1] + dy) % 4) * 2 + (pos[2] + dl) % 2
                 c = ((pos[0] + dx) % 4) * 8 + offset
@@ -321,7 +321,7 @@
     for piece in range(5, 9):
         scatter(piece)
     for part in range(3):
-        stage3(part, 1, 3)
+        stage3(part, 1)
     for stage, (took, gave) in enumerate(((x1, x2), (x2, x3))):
         for piece in range(9):
             axis = ORDERS[piece % 3][stage + 1]
@@ -331,6 +331,9 @@
             for step in (2, 1, 3):
                 remote(here, here, xs.at[stage + 1, piece], xr.at[stage + 1, piece], beside(axis, step))
             sent.append((gave[piece].at[0:3], xs.at[stage + 1, piece]))
+        if stage == 0:
+            for part in range(3):
+                stage3(part, 3)
     early = list(sent)
     sent.clear()
     for piece in range(9):

time: 69.4 us -> 69.4 us (level)
  no operation moved by 1% of the time
where the time goes in v8:
time: 69.4 us; the launch traced here: 69.3 us
  Pallas kernels  66.6 us (96%)
  local copies, waits for them, and re-layouts  2.01 us (3%)
    pallas_call x1, Pallas kernels, body(): pl.pallas_call(kernel, out_shape=(pltpu.VMEM((128, 512), F32), pltpu.VMEM...  66.6 us
    unnamed x2, local copies, waits for them, and re-layouts  2.01 us

profile of v8, /device:TPU:1, one launch (start us, length us, event | category | flops | bytes accessed | tf_op | source)
XLA Modules:
  0.0 69.3 jit_solution(9195365330537860081)
XLA Ops:
  0.6 66.6 %shard_map.86 = (f32[128,512]{1,0:T(8,128)S(1)}, f32[512,512]{1,0:T(8,128)S(1)}) custom-call(s32[1,1,32]{2,1,0:T(1,128)} %bitcast.6, s32[1,1,32]{2,1,0:T(1,128)} %bitcast.7, s32[1,1,32]{2,1,0:T(1,128)} %counts_ref.1, bf16[32,256,256]{2,1,0:T(8,128)(2,1)} %bitcast.5, bf16[512,512]{1,0:T(8,128)(2,1)} %g_any.1, bf16[128,512]{1,0:T(8,128)(2,1)} %x_any.1, ...), custom_call_target="tpu_custom_call" | custom-call | tf_op jit(solution)/shard_map/pallas_call | solution.py:437
  67.2 0.7 %copy.11 = f32[128,512]{1,0:T(8,128)} copy(f32[128,512]{1,0:T(8,128)S(1)} %get-tuple-element.8) | data formatting | bytes 524288
  67.9 1.3 %copy.9 = f32[512,512]{1,0:T(8,128)} copy(f32[512,512]{0,1:T(8,128)S(1)} %bitcast.4) | data formatting | bytes 2097152
